TPU v7x, 32 devices: a whole 2x2x4 slice. The times are simulated.
32 devices in a mesh: dp: 8 (over z, y), tensor: 4 (over x, core).
Axes of the slice: x: 2, y: 2, z: 4, core: 2. Of those that a mesh axis runs over, the one named last changes fastest.
Arguments:
- inputs: bfloat16 [8192, 768], P(('dp', 'tensor')), may hold values from -6 to 6
- cotangent: bfloat16 [8192, 768], P(('dp', 'tensor')), may hold values from -6 to 6
- norm_gains: bfloat16 [2, 2, 768], replicated, may hold values from 0.099609375 to 1.8984375
- in_weight: bfloat16 [2, 2, 768, 384], P(None, None, None, 'tensor'), may hold values from -0.21875 to 0.21875
- forget_weight: bfloat16 [2, 768, 384], P(None, None, 'tensor'), may hold values from -0.21875 to 0.21875
- gate_weight: bfloat16 [2, 2, 768, 384], P(None, None, None, 'tensor'), may hold values from -0.21875 to 0.21875
- out_weight: bfloat16 [2, 2, 384, 768], P(None, None, 'tensor'), may hold values from -0.3125 to 0.3125
- phase: float32 [2, 384], P(None, 'tensor'), may hold values from -3.140625 to 3.140625
- bound_logit: float32 [2, 384], P(None, 'tensor'), may hold values from -3 to 3
- group_gain: bfloat16 [2, 2, 384], P(None, None, 'tensor'), may hold values from 0.099609375 to 1.8984375
- ffn_weight: bfloat16 [2, 2, 768, 1536], P(None, None, None, 'tensor'), may hold values from -0.21875 to 0.21875
- down_weight: bfloat16 [2, 1536, 768], P(None, 'tensor'), may hold values from -0.21875 to 0.21875
Outputs:
- outputs: bfloat16 [8192, 768], P(('dp', 'tensor'))
- input_grad: bfloat16 [8192, 768], P(('dp', 'tensor'))
- norm_gains_grad: float32 [2, 2, 768], P(None, None, 'tensor')
- in_weight_grad: float32 [2, 2, 768, 384], P(None, None, None, 'tensor')
- forget_weight_grad: float32 [2, 768, 384], P(None, None, 'tensor')
- gate_weight_grad: float32 [2, 2, 768, 384], P(None, None, None, 'tensor')
- out_weight_grad: float32 [2, 2, 384, 768], P(None, None, 'tensor')
- phase_grad: float32 [2, 384], P(None, 'tensor')
- bound_logit_grad: float32 [2, 384], P(None, 'tensor')
- group_gain_grad: float32 [2, 2, 384], P(None, None, 'tensor')
- ffn_weight_grad: float32 [2, 2, 768, 1536], P(None, None, None, 'tensor')
- down_weight_grad: float32 [2, 1536, 768], P(None, 'tensor')
All inputs are finite; a program needn't handle non-finite values.
Results may differ from a plain program's by a relative error of at most 0.029.
Values may be sent and summed in bfloat16 or wider, within the bound.
A program may use at most 128 MiB of HBM per device.

v0:
```python
import jax
import jax.numpy as jnp
from jax import lax
from jax.sharding import PartitionSpec as P

GROUP_CH = 48


eps_norm = 1e-06
eps_group = 1e-05


def block_tables(angle_row):
    block_len = 64
    places = jnp.arange(block_len, dtype=jnp.float32)
    lag = places[:, None] - places[None, :]
    rot_cos = jnp.cos(lag[:, :, None] * angle_row)
    rot_sin = jnp.sin(lag[:, :, None] * angle_row)
    return (block_len, places, lag, rot_cos, rot_sin)


def forward_states(keep_rate, angle_row, drive_re, drive_im):
    length, channels = keep_rate.shape
    block_len, places, lag, rot_cos, rot_sin = block_tables(angle_row)
    blocks = length // block_len
    lead_cos = jnp.cos((places + 1.0)[:, None] * angle_row)
    lead_sin = jnp.sin((places + 1.0)[:, None] * angle_row)
    below = (lag >= 0.0)[:, :, None]
    shape3 = (blocks, block_len, channels)
    pieces_all = (
        jnp.log(keep_rate).reshape(shape3),
        drive_re.reshape(shape3),
        drive_im.reshape(shape3),
    )

    def advance(carry_state, pieces):
        log_keep, piece_re, piece_im = pieces
        running = jnp.cumsum(log_keep, axis=0)
        expo = jnp.where(below, running[:, None, :] - running[None, :, :], -jnp.inf)
        weight = jnp.exp(expo)
        weight_cos = weight * rot_cos
        weight_sin = weight * rot_sin
        state_re = jnp.sum(weight_cos * piece_re[None] - weight_sin * piece_im[None], axis=1)
        state_im = jnp.sum(weight_cos * piece_im[None] + weight_sin * piece_re[None], axis=1)
        decay = jnp.exp(running)
        carry_re, carry_im = carry_state
        state_re = state_re + decay * (lead_cos * carry_re - lead_sin * carry_im)
        state_im = state_im + decay * (lead_cos * carry_im + lead_sin * carry_re)
        return ((state_re[-1], state_im[-1]), (state_re, state_im))

    start_state = (jnp.zeros((channels,), jnp.float32), jnp.zeros((channels,), jnp.float32))
    final_state, states = lax.scan(advance, start_state, pieces_all)
    return (states[0].reshape(length, channels), states[1].reshape(length, channels))


def backward_totals(keep_rate, angle_row, grad_re, grad_im):
    length, channels = keep_rate.shape
    block_len, places, lag, rot_cos, rot_sin = block_tables(angle_row)
    blocks = length // block_len
    tail_cos = jnp.cos((block_len - 1.0 - places)[:, None] * angle_row)
    tail_sin = jnp.sin((block_len - 1.0 - places)[:, None] * angle_row)
    step_cos = jnp.cos(angle_row)
    step_sin = jnp.sin(angle_row)
    above = (lag <= 0.0)[:, :, None]
    shape3 = (blocks, block_len, channels)
    pieces_all = (
        jnp.log(keep_rate).reshape(shape3),
        grad_re.reshape(shape3),
        grad_im.reshape(shape3),
    )

    def retreat(carry_state, pieces):
        log_keep, piece_re, piece_im = pieces
        running = jnp.cumsum(log_keep, axis=0)
        expo = jnp.where(above, running[None, :, :] - running[:, None, :], -jnp.inf)
        weight = jnp.exp(expo)
        weight_cos = weight * rot_cos
        weight_sin = weight * rot_sin
        total_re = jnp.sum(weight_cos * piece_re[None] - weight_sin * piece_im[None], axis=1)
        total_im = jnp.sum(weight_cos * piece_im[None] + weight_sin * piece_re[None], axis=1)
        decay = jnp.exp(running[-1][None, :] - running)
        carry_re, carry_im = carry_state
        total_re = total_re + decay * (tail_cos * carry_re + tail_sin * carry_im)
        total_im = total_im + decay * (tail_cos * carry_im - tail_sin * carry_re)
        first_keep = jnp.exp(log_keep[0])
        next_re = first_keep * (step_cos * total_re[0] + step_sin * total_im[0])
        next_im = first_keep * (step_cos * total_im[0] - step_sin * total_re[0])
        return ((next_re, next_im), (total_re, total_im))

    start_state = (jnp.zeros((channels,), jnp.float32), jnp.zeros((channels,), jnp.float32))
    final_state, totals = lax.scan(retreat, start_state, pieces_all, reverse=True)
    return (totals[0].reshape(length, channels), totals[1].reshape(length, channels))


def norm_apply(stream, gain_row):
    inv_scale = lax.rsqrt(jnp.mean(stream * stream, axis=-1, keepdims=True) + eps_norm)
    return (stream * inv_scale * gain_row, inv_scale)


def norm_back(stream, inv_scale, gain_row, grad_out):
    gain_grad = jnp.sum(grad_out * stream * inv_scale, axis=0)
    grad_scaled = grad_out * gain_row
    grad_input = inv_scale * grad_scaled - stream * inv_scale * inv_scale * inv_scale * jnp.mean(
        grad_scaled * stream, axis=-1, keepdims=True
    )
    return (grad_input, gain_grad)


def group_stats(state_re, state_im):
    length, channels = state_re.shape
    grid_shape = (length, channels // GROUP_CH, GROUP_CH)
    grouped_re = state_re.reshape(grid_shape)
    grouped_im = state_im.reshape(grid_shape)
    centre = (
        jnp.sum(grouped_re, axis=-1, keepdims=True) + jnp.sum(grouped_im, axis=-1, keepdims=True)
    ) / (2 * GROUP_CH)
    dev_re = grouped_re - centre
    dev_im = grouped_im - centre
    spread = (
        jnp.sum(dev_re * dev_re, axis=-1, keepdims=True)
        + jnp.sum(dev_im * dev_im, axis=-1, keepdims=True)
    ) / (2 * GROUP_CH)
    inv_scale = lax.rsqrt(spread + eps_group)
    return (
        (dev_re * inv_scale).reshape(length, channels),
        (dev_im * inv_scale).reshape(length, channels),
        inv_scale,
    )


def group_back(grad_re, grad_im, unit_re, unit_im, inv_scale):
    length, channels = grad_re.shape
    grid_shape = (length, channels // GROUP_CH, GROUP_CH)
    grid_gre = grad_re.reshape(grid_shape)
    grid_gim = grad_im.reshape(grid_shape)
    grid_ure = unit_re.reshape(grid_shape)
    grid_uim = unit_im.reshape(grid_shape)
    mean_grad = (
        jnp.sum(grid_gre, axis=-1, keepdims=True) + jnp.sum(grid_gim, axis=-1, keepdims=True)
    ) / (2 * GROUP_CH)
    mean_cross = (
        jnp.sum(grid_gre * grid_ure, axis=-1, keepdims=True)
        + jnp.sum(grid_gim * grid_uim, axis=-1, keepdims=True)
    ) / (2 * GROUP_CH)
    back_re = inv_scale * (grid_gre - mean_grad - grid_ure * mean_cross)
    back_im = inv_scale * (grid_gim - mean_grad - grid_uim * mean_cross)
    return (back_re.reshape(length, channels), back_im.reshape(length, channels))


def contract_rows(left, right):
    return lax.dot_general(
        left, right, (((0,), (0,)), ((), ())), preferred_element_type=jnp.float32
    )


def contract_cols(left, right):
    return lax.dot_general(
        left, right, (((1,), (1,)), ((), ())), preferred_element_type=jnp.float32
    )


def local(
    inputs,
    cotangent,
    norm_gains,
    in_weight,
    forget_weight,
    gate_weight,
    out_weight,
    phase,
    bound_logit,
    group_gain,
    ffn_weight,
    down_weight,
):
    layers = norm_gains.shape[0]
    channels = forget_weight.shape[2]
    hidden_width = down_weight.shape[1]
    model_width = inputs.shape[1]
    stream = inputs.astype(jnp.float32)
    records = []
    for layer_idx in range(layers):
        norm_gain = norm_gains[layer_idx].astype(jnp.float32)
        normed, scale_mix = norm_apply(stream, norm_gain[0])
        mix_full = lax.all_gather(normed.astype(jnp.bfloat16), "tensor", axis=0, tiled=True)
        mix_mats = (
            in_weight[layer_idx, 0],
            in_weight[layer_idx, 1],
            forget_weight[layer_idx],
            gate_weight[layer_idx, 0],
            gate_weight[layer_idx, 1],
        )
        in_re, in_im, forget_pre, gate_re_pre, gate_im_pre = tuple(
            (jnp.dot(mix_full, matrix, preferred_element_type=jnp.float32) for matrix in mix_mats)
        )
        lower_bound = jax.nn.sigmoid(bound_logit[layer_idx])
        forget_sig = jax.nn.sigmoid(forget_pre)
        keep_rate = lower_bound + (1.0 - lower_bound) * forget_sig
        state_re, state_im = forward_states(
            keep_rate,
            phase[layer_idx],
            (1.0 - keep_rate) * jax.nn.silu(in_re),
            (1.0 - keep_rate) * jax.nn.silu(in_im),
        )
        unit_re, unit_im, scale_group = group_stats(state_re, state_im)
        group_pair = group_gain[layer_idx].astype(jnp.float32)
        sig_gate_re = jax.nn.sigmoid(gate_re_pre)
        sig_gate_im = jax.nn.sigmoid(gate_im_pre)
        mixed_re = (unit_re * group_pair[0] * sig_gate_re).astype(jnp.bfloat16)
        mixed_im = (unit_im * group_pair[1] * sig_gate_im).astype(jnp.bfloat16)
        out_re = out_weight[layer_idx, 0]
        out_im = out_weight[layer_idx, 1]
        stream_mid = stream + lax.psum_scatter(
            (
                jnp.dot(mixed_re, out_re, preferred_element_type=jnp.float32)
                + jnp.dot(mixed_im, out_im, preferred_element_type=jnp.float32)
            ).astype(jnp.bfloat16),
            "tensor",
            scatter_dimension=0,
            tiled=True,
        ).astype(jnp.float32)
        normed_ffn, scale_ffn = norm_apply(stream_mid, norm_gain[1])
        ffn_full = lax.all_gather(normed_ffn.astype(jnp.bfloat16), "tensor", axis=0, tiled=True)
        ffn_cat = jnp.concatenate([ffn_weight[layer_idx, 0], ffn_weight[layer_idx, 1]], axis=1)
        gate_up = jnp.dot(ffn_full, ffn_cat, preferred_element_type=jnp.float32)
        hidden = (jax.nn.silu(gate_up[:, :hidden_width]) * gate_up[:, hidden_width:]).astype(
            jnp.bfloat16
        )
        down_mat = down_weight[layer_idx]
        stream_next = stream_mid + lax.psum_scatter(
            jnp.dot(hidden, down_mat, preferred_element_type=jnp.float32).astype(jnp.bfloat16),
            "tensor",
            scatter_dimension=0,
            tiled=True,
        ).astype(jnp.float32)
        records.append(
            (
                stream,
                scale_mix,
                mix_full,
                mix_mats,
                in_re,
                in_im,
                forget_sig,
                keep_rate,
                sig_gate_re,
                sig_gate_im,
                state_re,
                state_im,
                unit_re,
                unit_im,
                scale_group,
                mixed_re,
                mixed_im,
                stream_mid,
                scale_ffn,
                ffn_full,
                ffn_cat,
                gate_up,
                hidden,
            )
        )
        stream = stream_next
    outputs = stream.astype(jnp.bfloat16)
    gradient = cotangent.astype(jnp.float32)
    collected = []
    gain_list = []
    for layer_idx in reversed(range(layers)):
        (
            stream_in,
            scale_mix,
            mix_full,
            mix_mats,
            in_re,
            in_im,
            forget_sig,
            keep_rate,
            sig_gate_re,
            sig_gate_im,
            state_re,
            state_im,
            unit_re,
            unit_im,
            scale_group,
            mixed_re,
            mixed_im,
            stream_mid,
            scale_ffn,
            ffn_full,
            ffn_cat,
            gate_up,
            hidden,
        ) = records[layer_idx]
        norm_gain = norm_gains[layer_idx].astype(jnp.float32)
        down_mat = down_weight[layer_idx]
        grad_full = lax.all_gather(gradient.astype(jnp.bfloat16), "tensor", axis=0, tiled=True)
        grad_hidden = contract_cols(grad_full, down_mat)
        grad_down = contract_rows(hidden, grad_full)
        gate_val = gate_up[:, :hidden_width]
        up_val = gate_up[:, hidden_width:]
        sig_val = jax.nn.sigmoid(gate_val)
        grad_up = grad_hidden * gate_val * sig_val
        grad_gate = grad_hidden * up_val * sig_val * (1.0 + gate_val * (1.0 - sig_val))
        grad_gate_up = jnp.concatenate([grad_gate, grad_up], axis=1).astype(jnp.bfloat16)
        grad_ffn_cat = contract_rows(ffn_full, grad_gate_up)
        grad_ffn_w = jnp.stack([grad_ffn_cat[:, :hidden_width], grad_ffn_cat[:, hidden_width:]])
        grad_norm_ffn = lax.psum_scatter(
            contract_cols(grad_gate_up, ffn_cat).astype(jnp.bfloat16),
            "tensor",
            scatter_dimension=0,
            tiled=True,
        ).astype(jnp.float32)
        grad_from_ffn, gain_ffn = norm_back(stream_mid, scale_ffn, norm_gain[1], grad_norm_ffn)
        gradient = gradient + grad_from_ffn
        grad_full = lax.all_gather(gradient.astype(jnp.bfloat16), "tensor", axis=0, tiled=True)
        out_re = out_weight[layer_idx, 0]
        out_im = out_weight[layer_idx, 1]
        grad_mixed_re = contract_cols(grad_full, out_re)
        grad_mixed_im = contract_cols(grad_full, out_im)
        grad_out_w = jnp.stack(
            [contract_rows(mixed_re, grad_full), contract_rows(mixed_im, grad_full)]
        )
        group_pair = group_gain[layer_idx].astype(jnp.float32)
        grad_normal_re = grad_mixed_re * sig_gate_re
        grad_normal_im = grad_mixed_im * sig_gate_im
        grad_gate_re = grad_mixed_re * unit_re * group_pair[0] * sig_gate_re * (1.0 - sig_gate_re)
        grad_gate_im = grad_mixed_im * unit_im * group_pair[1] * sig_gate_im * (1.0 - sig_gate_im)
        grad_group = jnp.stack(
            [jnp.sum(grad_normal_re * unit_re, axis=0), jnp.sum(grad_normal_im * unit_im, axis=0)]
        )
        grad_state_re, grad_state_im = group_back(
            grad_normal_re * group_pair[0],
            grad_normal_im * group_pair[1],
            unit_re,
            unit_im,
            scale_group,
        )
        lower_bound = jax.nn.sigmoid(bound_logit[layer_idx])
        cosine = jnp.cos(phase[layer_idx])
        sine_part = jnp.sin(phase[layer_idx])
        total_re, total_im = backward_totals(
            keep_rate, phase[layer_idx], grad_state_re, grad_state_im
        )
        zero_row = jnp.zeros((1, channels), jnp.float32)
        prev_re = jnp.concatenate([zero_row, state_re[:-1]], axis=0)
        prev_im = jnp.concatenate([zero_row, state_im[:-1]], axis=0)
        grad_coeff_re = total_re * prev_re + total_im * prev_im
        grad_coeff_im = total_im * prev_re - total_re * prev_im
        sig_in_re = jax.nn.sigmoid(in_re)
        sig_in_im = jax.nn.sigmoid(in_im)
        grad_keep = (
            grad_coeff_re * cosine
            + grad_coeff_im * sine_part
            - (total_re * in_re * sig_in_re + total_im * in_im * sig_in_im)
        )
        grad_phase = jnp.sum(
            keep_rate * (grad_coeff_im * cosine - grad_coeff_re * sine_part), axis=0
        )
        grad_bound = (
            jnp.sum(grad_keep * (1.0 - forget_sig), axis=0) * lower_bound * (1.0 - lower_bound)
        )
        grad_in_re = total_re * (1.0 - keep_rate) * sig_in_re * (1.0 + in_re * (1.0 - sig_in_re))
        grad_in_im = total_im * (1.0 - keep_rate) * sig_in_im * (1.0 + in_im * (1.0 - sig_in_im))
        grad_forget = grad_keep * (1.0 - lower_bound) * forget_sig * (1.0 - forget_sig)
        grad_parts = tuple(
            (
                part.astype(jnp.bfloat16)
                for part in (grad_in_re, grad_in_im, grad_forget, grad_gate_re, grad_gate_im)
            )
        )
        weight_parts = tuple((contract_rows(mix_full, part) for part in grad_parts))
        grad_in_w = jnp.stack([weight_parts[0], weight_parts[1]])
        grad_forget_w = weight_parts[2]
        grad_gate_w = jnp.stack([weight_parts[3], weight_parts[4]])
        summed_rows = None
        for mix_part, mix_matrix in zip(grad_parts, mix_mats):
            term = contract_cols(mix_part, mix_matrix)
            summed_rows = term if summed_rows is None else summed_rows + term
        grad_norm_mix = lax.psum_scatter(
            summed_rows.astype(jnp.bfloat16), "tensor", scatter_dimension=0, tiled=True
        ).astype(jnp.float32)
        grad_from_mix, gain_mix = norm_back(stream_in, scale_mix, norm_gain[0], grad_norm_mix)
        gradient = gradient + grad_from_mix
        gain_list.append(jnp.stack([gain_mix, gain_ffn]))
        layer_grads = (
            grad_in_w,
            grad_forget_w,
            grad_gate_w,
            grad_out_w,
            grad_phase,
            grad_bound,
            grad_group,
            grad_ffn_w,
            grad_down,
        )
        collected.append(layer_grads)
    ordered = collected[::-1]
    stacked = tuple(
        (jnp.stack([grads_layer[position] for grads_layer in ordered]) for position in range(9))
    )
    summed = lax.psum(
        (
            stacked[0],
            stacked[1],
            stacked[2],
            stacked[3],
            stacked[4],
            stacked[5],
            stacked[6],
            stacked[7],
            stacked[8],
        ),
        "dp",
    )
    gain_stack = jnp.stack(gain_list[::-1])
    gain_total = lax.psum(gain_stack, ("dp", "tensor"))
    gain_piece = model_width // lax.axis_size("tensor")
    gain_slice = lax.dynamic_slice_in_dim(
        gain_total, lax.axis_index("tensor") * gain_piece, gain_piece, 2
    )
    return (
        outputs,
        gradient.astype(jnp.bfloat16),
        gain_slice,
        summed[0],
        summed[1],
        summed[2],
        summed[3],
        summed[4],
        summed[5],
        summed[6],
        summed[7],
        summed[8],
    )


def solution(mesh):
    return jax.shard_map(
        local,
        mesh=mesh,
        in_specs=(
            P(("dp", "tensor"), None),
            P(("dp", "tensor"), None),
            P(),
            P(None, None, None, "tensor"),
            P(None, None, "tensor"),
            P(None, None, None, "tensor"),
            P(None, None, "tensor", None),
            P(None, "tensor"),
            P(None, "tensor"),
            P(None, None, "tensor"),
            P(None, None, None, "tensor"),
            P(None, "tensor", None),
        ),
        out_specs=(
            P(("dp", "tensor"), None),
            P(("dp", "tensor"), None),
            P(None, None, "tensor"),
            P(None, None, None, "tensor"),
            P(None, None, "tensor"),
            P(None, None, None, "tensor"),
            P(None, None, "tensor", None),
            P(None, "tensor"),
            P(None, "tensor"),
            P(None, None, "tensor"),
            P(None, None, None, "tensor"),
            P(None, "tensor", None),
        ),
        check_vma=False,
    )
```

profile of v0, /device:TPU:0, one launch (start us, length us, event | category | flops | bytes accessed | tf_op | source)
XLA Modules:
  0.0 2118.6 jit_solution(2739337086760076813)
XLA Ops:
  15.3 19.5 all-gather.9.cloned.1.call-done
  42.7 175.7 %while.82 = (s32[]{:T(128)}, f32[96]{0:T(128)S(1)}, f32[96]{0:T(128)S(1)}, f32[16,64,96]{2,1,0:T(8,128)S(1)}, f32[16,64,96]{2,1,0:T(8,128)S(1)}, /*index=5*/f32[...) while((s32[]{:T(128)}, f32[96]{0:T(128)S(1)}, ...), condition=%wide.region_5.6_spmd.clone.clone, body=%wide.region_1.5_spmd.clone.clone.sunk | while | flops 5569474 | bytes 614421 | solution.py:52
  236.3 28.3 %reduce-scatter.9.cloned.1.call-done = bf16[256,768]{1,0:T(8,128)(2,1)} async-done(((bf16[1024,768]{1,0:T(8,128)(2,1)}), bf16[256,768]{1,0:T(8,128)(2,1)}) %reduce-scatter.9.cloned.1.call-update) | async-done | bytes 393232 | tf_op jit(solution)/shard_map/reduce_scatter | solution.py:213
  270.6 16.9 all-gather.11.cloned.1.call-done
  296.1 27.0 %reduce-scatter.11.cloned.1.call-done = bf16[256,768]{1,0:T(8,128)(2,1)} async-done(((bf16[1024,768]{1,0:T(8,128)(2,1)}), bf16[256,768]{1,0:T(8,128)(2,1)}) %reduce-scatter.11.cloned.1.call-update) | async-done | bytes 393232 | tf_op jit(solution)/shard_map/reduce_scatter | solution.py:230
  326.2 18.9 all-gather.13.cloned.1.call-done
  358.6 316.1 %while.83 = (s32[]{:T(128)}, f32[96]{0:T(128)}, f32[96]{0:T(128)}, f32[16,64,96]{2,1,0:T(8,128)}, f32[16,64,96]{2,1,0:T(8,128)}, /*index=5*/f32[16,64,96]{2,1,0:...) while((s32[]{:T(128)}, f32[96]{0:T(128)}, f32[96]{0:T(128)}, ...), condition=%wide.region_18.19_spmd.clone.clone, body=%wide.region_14.18_spmd.clone.clone.sunk | while | flops 5569474 | bytes 690665 | solution.py:52
  366.1 10.7 add_reduce_fusion.7
  385.9 10.7 add_reduce_fusion.7
  405.6 10.7 add_reduce_fusion.7
  425.4 10.7 add_reduce_fusion.7
  445.2 10.7 add_reduce_fusion.7
  464.9 10.7 add_reduce_fusion.7
  484.7 10.7 add_reduce_fusion.7
  504.4 10.7 add_reduce_fusion.7
  524.2 10.7 add_reduce_fusion.7
  543.9 10.7 add_reduce_fusion.7
  563.7 10.7 add_reduce_fusion.7
  583.5 10.7 add_reduce_fusion.7
  603.2 10.7 add_reduce_fusion.7
  623.0 10.7 add_reduce_fusion.7
  642.7 10.7 add_reduce_fusion.7
  662.5 10.7 add_reduce_fusion.7
  699.5 28.3 %reduce-scatter.13.cloned.1.call-done = bf16[256,768]{1,0:T(8,128)(2,1)} async-done(((bf16[1024,768]{1,0:T(8,128)(2,1)}), bf16[256,768]{1,0:T(8,128)(2,1)}) %reduce-scatter.13.cloned.1.call-update) | async-done | bytes 393232 | tf_op jit(solution)/shard_map/reduce_scatter | solution.py:213
  732.6 19.0 all-gather.15.cloned.1.call-done
  756.4 16.5 all-gather.17.cloned.1.call-done
  782.0 27.8 %reduce-scatter.17.cloned.1.call-done = bf16[256,768]{1,0:T(8,128)(2,1)} async-done(((bf16[1024,768]{1,0:T(8,128)(2,1)}), bf16[256,768]{1,0:T(8,128)(2,1)}) %reduce-scatter.17.cloned.1.call-update) | async-done | bytes 393232 | tf_op jit(solution)/shard_map/reduce_scatter | solution.py:307
  823.5 11.3 all-gather.19.cloned.1.call-done
  868.5 326.3 %while.84 = (s32[]{:T(128)}, f32[96]{0:T(128)}, f32[96]{0:T(128)}, f32[16,64,96]{2,1,0:T(8,128)}, f32[16,64,96]{2,1,0:T(8,128)}, /*index=5*/f32[16,64,96]{2,1,0:...) while((s32[]{:T(128)}, f32[96]{0:T(128)}, f32[96]{0:T(128)}, ...), condition=%wide.region_36.37_spmd.clone.clone.clone, body=%wide.region_32.36_spmd.clone.clone.clone.sunk | while | flops 5582724 | bytes 699231 | solution.py:91
  874.1 10.7 subtract_reduce_fusion.6
  894.5 10.7 subtract_reduce_fusion.6
  914.9 10.7 subtract_reduce_fusion.6
  935.4 10.7 subtract_reduce_fusion.6
  955.8 10.7 subtract_reduce_fusion.6
  976.2 10.7 subtract_reduce_fusion.6
  996.7 10.7 subtract_reduce_fusion.6
  1017.1 10.7 subtract_reduce_fusion.6
  1037.5 10.7 subtract_reduce_fusion.6
  1058.0 10.7 subtract_reduce_fusion.6
  1078.4 10.7 subtract_reduce_fusion.6
  1098.8 10.7 subtract_reduce_fusion.6
  1119.3 10.7 subtract_reduce_fusion.6
  1139.7 10.7 subtract_reduce_fusion.6
  1160.1 10.7 subtract_reduce_fusion.6
  1180.6 10.7 subtract_reduce_fusion.6
  1211.5 24.5 %reduce-scatter.19.cloned.1.call-done = bf16[256,768]{1,0:T(8,128)(2,1)} async-done(((bf16[1024,768]{1,0:T(8,128)(2,1)}), bf16[256,768]{1,0:T(8,128)(2,1)}) %reduce-scatter.19.cloned.1.call-update) | async-done | bytes 393232 | tf_op jit(solution)/shard_map/reduce_scatter | solution.py:379
  1238.7 28.7 %reduce-scatter.15.cloned.1.call-done = bf16[256,768]{1,0:T(8,128)(2,1)} async-done(((bf16[1024,768]{1,0:T(8,128)(2,1)}), bf16[256,768]{1,0:T(8,128)(2,1)}) %reduce-scatter.15.cloned.1.call-update) | async-done | bytes 393232 | tf_op jit(solution)/shard_map/reduce_scatter | solution.py:230
  1271.0 19.8 all-gather.21.cloned.1.call-done
  1310.2 16.5 reduce-scatter.21.cloned.1.call-done
  1385.0 318.1 %while.85 = (s32[]{:T(128)}, f32[96]{0:T(128)}, f32[96]{0:T(128)}, f32[16,64,96]{2,1,0:T(8,128)}, f32[16,64,96]{2,1,0:T(8,128)}, /*index=5*/f32[16,64,96]{2,1,0:...) while((s32[]{:T(128)}, f32[96]{0:T(128)}, f32[96]{0:T(128)}, ...), condition=%wide.region_49.50_spmd.clone.clone.clone, body=%wide.region_45.49_spmd.clone.clone.clone.sunk | while | flops 5582724 | bytes 699231 | solution.py:91
  1390.2 10.6 subtract_reduce_fusion.7
  1410.1 10.6 subtract_reduce_fusion.7
  1430.0 10.6 subtract_reduce_fusion.7
  1449.9 10.6 subtract_reduce_fusion.7
  1469.9 10.6 subtract_reduce_fusion.7
  1489.8 10.6 subtract_reduce_fusion.7
  1509.7 10.6 subtract_reduce_fusion.7
  1529.6 10.6 subtract_reduce_fusion.7
  1549.5 10.6 subtract_reduce_fusion.7
  1569.4 10.6 subtract_reduce_fusion.7
  1589.3 10.6 subtract_reduce_fusion.7
  1734.5 22.0 %all-reduce.4 = (f32[2,96]{1,0:T(2,128)}, f32[2,96]{1,0:T(2,128)}, f32[2,2,96]{2,1,0:T(2,128)}) all-reduce(f32[2,96]{1,0:T(2,128)S(1)} %pad_maximum_fusion.20, f32[2,96]{1,0:T(2,128)S(1)} %pad_maximum_fusion.21, f32[2,2,96]{2,1,0:T(2,128)S(1)} %pad_maximum_fusion.19), channel_id=1, replica_groups=mesh['dp'=8,'tensor'=4] {'dp'}, use_global_device_ids=true, to_apply=%region_63.64 | all-reduce | flops 768 | bytes 6144 | tf_op jit(solution)/shard_map/psum | solution.py:401
  1757.9 42.7 %psum.70 = f32[2,2,768]{2,1,0:T(2,128)S(1)} all-reduce(f32[2,2,768]{2,1,0:T(2,128)S(1)} %pad_maximum_fusion.18), channel_id=1, replica_groups=mesh['dp'=8,'tensor'=4] {'dp','tensor'}, use_global_device_ids=true, to_apply=%region_56.57 | all-reduce | flops 3072 | bytes 24576 | tf_op jit(solution)/shard_map/psum | solution.py:416
  1803.7 297.3 %all-reduce.8.cloned.1.call-done = (f32[2,2,768,96]{2,3,1,0:T(8,128)}, f32[2,768,96]{1,2,0:T(8,128)}, f32[2,2,768,96]{2,3,1,0:T(8,128)}, f32[2,2,96,768]{3,2,1,0...) async-done(((f32[2,2,768,96]{2,3,1,0:T(8,128)}, f32[2,768,96]{1,2,0:T(8,128)}, f32[2,2,768,96]{2,3,1,0:T(8,128)}, f32[2,2,96,768]{3,2,1,0:T(8,128)}, ...) | async-done | bytes 11206672 | tf_op jit(solution)/shard_map/psum | solution.py:401
  (1650 shorter events, 974.8 us)
Async XLA Ops:
  7.2 27.6 %copy-start.94 = (bf16[2,768,96]{1,2,0:T(8,128)(2,1)S(1)}, bf16[2,768,96]{1,2,0:T(8,128)(2,1)}, u32[]{:S(2)}) copy-start(bf16[2,768,96]{1,2,0:T(8,128)(2,1)} %param.24) | copy-start | bytes 884740
  7.2 27.6 %all-gather.9.cloned.1.call-start = ((), (), s32[]{:S(2)}) async-start(), calls=%async_computation.8 | async-start | bytes 1966080 | tf_op jit(solution)/shard_map/all_gather | solution.py:185
  8.5 26.4 %copy-start.132 = (f32[256]{0:T(256)}, f32[256]{0:T(256)S(1)}, u32[]{:S(2)}) copy-start(f32[256]{0:T(256)S(1)} %add_rsqrt_fusion.5) | copy-start | bytes 3076
  10.4 24.4 %copy-start.115 = (f32[768]{0:T(1024)}, f32[768]{0:T(1024)S(1)}, u32[]{:S(2)}) copy-start(f32[768]{0:T(1024)S(1)} %get-tuple-element.1329) | copy-start | bytes 9220
  12.3 252.2 %reduce-scatter.9.cloned.1.call-start = ((), (), s32[]{:S(2)}) async-start(), calls=%async_computation.9 | async-start | bytes 1966080 | tf_op jit(solution)/shard_map/reduce_scatter | solution.py:213
  13.6 24.0 %copy-start.141 = (f32[96]{0:T(128)}, f32[96]{0:T(128)S(1)}, u32[]{:S(2)}) copy-start(f32[96]{0:T(128)S(1)} %get-tuple-element.1545) | copy-start | bytes 1156
  13.6 24.1 %copy-start.155 = (f32[1,96]{1,0:T(1,128)}, f32[1,96]{1,0:T(1,128)S(1)}, u32[]{:S(2)}) copy-start(f32[1,96]{1,0:T(1,128)S(1)} %get-tuple-element.1546) | copy-start | bytes 1156
  15.3 21.7 %copy-start.75 = (bf16[2,2,768,96]{2,3,1,0:T(8,128)(2,1)S(1)}, bf16[2,2,768,96]{2,3,1,0:T(8,128)(2,1)}, u32[]{:S(2)}) copy-start(bf16[2,2,768,96]{2,3,1,0:T(8,128)(2,1)} %param.23) | copy-start | bytes 1769476
  236.2 28.3 %copy-start.5 = (bf16[256,768]{1,0:T(8,128)(2,1)S(1)}, bf16[256,768]{1,0:T(8,128)(2,1)}, u32[]{:S(2)}) copy-start(bf16[256,768]{1,0:T(8,128)(2,1)} %param.20) | copy-start | bytes 1179652
  236.2 29.6 %copy-start.110 = (f32[768]{0:T(1024)S(1)}, f32[768]{0:T(1024)}, u32[]{:S(2)}) copy-start(f32[768]{0:T(1024)} %get-tuple-element.1328) | copy-start | bytes 9220
  236.2 51.3 %all-gather.11.cloned.1.call-start = ((), (), s32[]{:S(2)}) async-start(), calls=%async_computation.10 | async-start | bytes 1966080 | tf_op jit(solution)/shard_map/all_gather | solution.py:223
  267.7 55.3 %reduce-scatter.11.cloned.1.call-start = ((), (), s32[]{:S(2)}) async-start(), calls=%async_computation.11 | async-start | bytes 1966080 | tf_op jit(solution)/shard_map/reduce_scatter | solution.py:230
  270.6 16.9 copy-start.86
  270.6 16.9 copy-start.88
  294.8 28.3 %copy-start.9 = (bf16[256,768]{1,0:T(8,128)(2,1)S(1)}, bf16[256,768]{1,0:T(8,128)(2,1)}, u32[]{:S(2)}) copy-start(bf16[256,768]{1,0:T(8,128)(2,1)} %reduce-scatter.9.cloned.1.call-done) | copy-start | bytes 1179652
  294.8 50.4 %all-gather.13.cloned.1.call-start = ((), (), s32[]{:S(2)}) async-start(), calls=%async_computation.12 | async-start | bytes 1966080 | tf_op jit(solution)/shard_map/all_gather | solution.py:185
  296.1 29.3 %copy-start.117 = (f32[768]{0:T(1024)}, f32[768]{0:T(1024)S(1)}, u32[]{:S(2)}) copy-start(f32[768]{0:T(1024)S(1)} %get-tuple-element.1326) | copy-start | bytes 9220
  296.1 29.6 %copy-start.157 = (f32[1,2,96]{2,1,0:T(2,128)S(1)}, f32[1,2,96]{2,1,0:T(2,128)}, u32[]{:S(2)}) copy-start(f32[1,2,96]{2,1,0:T(2,128)} %get-tuple-element.1543) | copy-start | bytes 2308
  325.4 402.4 %reduce-scatter.13.cloned.1.call-start = ((), (), s32[]{:S(2)}) async-start(), calls=%async_computation.13 | async-start | bytes 1966080 | tf_op jit(solution)/shard_map/reduce_scatter | solution.py:213
  364.5 12.5 copy-start.122
  364.5 12.5 copy-start.123
  384.2 12.5 copy-start.123
  404.0 12.5 copy-start.122
  404.0 12.5 copy-start.123
  423.8 12.5 copy-start.122
  423.8 12.5 copy-start.123
  443.5 12.5 copy-start.123
  463.3 12.5 copy-start.123
  483.0 12.5 copy-start.122
  483.0 12.5 copy-start.123
  502.8 12.5 copy-start.122
  502.8 12.5 copy-start.123
  522.6 12.5 copy-start.123
  542.3 12.5 copy-start.123
  562.1 12.5 copy-start.122
  562.1 12.5 copy-start.123
  581.8 12.5 copy-start.122
  581.8 12.5 copy-start.123
  601.6 12.5 copy-start.123
  621.3 12.5 copy-start.123
  641.1 12.5 copy-start.122
  641.1 12.5 copy-start.123
  660.9 12.5 copy-start.123
  699.5 52.1 %all-gather.15.cloned.1.call-start = ((), (), s32[]{:S(2)}) async-start(), calls=%async_computation.14 | async-start | bytes 1966080 | tf_op jit(solution)/shard_map/all_gather | solution.py:223
  731.8 41.1 %all-gather.17.cloned.1.call-start = ((), (), s32[]{:S(2)}) async-start(), calls=%async_computation.16 | async-start | bytes 1966080 | tf_op jit(solution)/shard_map/all_gather | solution.py:296
  732.5 77.3 %reduce-scatter.17.cloned.1.call-start = ((), (), s32[]{:S(2)}) async-start(), calls=%async_computation.17 | async-start | bytes 1966080 | tf_op jit(solution)/shard_map/reduce_scatter | solution.py:307
  781.5 53.3 %all-gather.19.cloned.1.call-start = ((), (), s32[]{:S(2)}) async-start(), calls=%async_computation.18 | async-start | bytes 1966080 | tf_op jit(solution)/shard_map/all_gather | solution.py:315
  815.0 421.1 %reduce-scatter.19.cloned.1.call-start = ((), (), s32[]{:S(2)}) async-start(), calls=%async_computation.19 | async-start | bytes 1966080 | tf_op jit(solution)/shard_map/reduce_scatter | solution.py:379
  1207.7 59.6 %reduce-scatter.15.cloned.1.call-start = ((), (), s32[]{:S(2)}) async-start(), calls=%async_computation.15 | async-start | bytes 1966080 | tf_op jit(solution)/shard_map/reduce_scatter | solution.py:230
  1211.3 56.1 %copy-start.114 = (f32[768]{0:T(1024)S(1)}, f32[768]{0:T(1024)}, u32[]{:S(2)}) copy-start(f32[768]{0:T(1024)} %get-tuple-element.1327) | copy-start | bytes 9220
  1211.3 79.5 %all-gather.21.cloned.1.call-start = ((), (), s32[]{:S(2)}) async-start(), calls=%async_computation.20 | async-start | bytes 1966080 | tf_op jit(solution)/shard_map/all_gather | solution.py:296
  1270.9 55.7 %reduce-scatter.21.cloned.1.call-start = ((), (), s32[]{:S(2)}) async-start(), calls=%async_computation.21 | async-start | bytes 1966080 | tf_op jit(solution)/shard_map/reduce_scatter | solution.py:307
  1298.3 53.1 %all-gather.23.cloned.1.call-start = ((), (), s32[]{:S(2)}) async-start(), calls=%async_computation.22 | async-start | bytes 1966080 | tf_op jit(solution)/shard_map/all_gather | solution.py:315
  1308.6 18.0 copy-start.111
  1331.6 424.9 %reduce-scatter.23.cloned.1.call-start = ((), (), s32[]{:S(2)}) async-start(), calls=%async_computation.23 | async-start | bytes 1966080 | tf_op jit(solution)/shard_map/reduce_scatter | solution.py:379
  1715.5 385.4 %all-reduce.8.cloned.1.call-start = ((), (), s32[]{:S(2)}) async-start(), calls=%async_computation.24 | async-start | bytes 22413312 | tf_op jit(solution)/shard_map/psum | solution.py:401
  1733.7 22.8 %copy-start.116 = (f32[768]{0:T(1024)S(1)}, f32[768]{0:T(1024)}, u32[]{:S(2)}) copy-start(f32[768]{0:T(1024)} %copy-done.115) | copy-start | bytes 9220
  1733.7 22.8 %copy-start.133 = (f32[256]{0:T(256)S(1)}, f32[256]{0:T(256)}, u32[]{:S(2)}) copy-start(f32[256]{0:T(256)} %copy-done.132) | copy-start | bytes 3076
  1733.7 67.5 %copy-start.10 = (bf16[256,768]{1,0:T(8,128)(2,1)S(1)}, bf16[256,768]{1,0:T(8,128)(2,1)}, u32[]{:S(2)}) copy-start(bf16[256,768]{1,0:T(8,128)(2,1)} %reduce-scatter.9.cloned.1.call-done) | copy-start | bytes 1179652
  1733.8 67.5 %copy-start.17 = (f32[256,768]{1,0:T(8,128)S(1)}, f32[256,768]{1,0:T(8,128)}, u32[]{:S(2)}) copy-start(f32[256,768]{1,0:T(8,128)} %get-tuple-element.1444) | copy-start | bytes 2359300
  1733.8 67.5 %copy-start.29 = (bf16[256,768]{1,0:T(8,128)(2,1)S(1)}, bf16[256,768]{1,0:T(8,128)(2,1)}, u32[]{:S(2)}) copy-start(bf16[256,768]{1,0:T(8,128)(2,1)} %reduce-scatter.21.cloned.1.call-done) | copy-start | bytes 1179652
  1733.8 67.5 %copy-start.112 = (f32[768]{0:T(1024)S(1)}, f32[768]{0:T(1024)}, u32[]{:S(2)}) copy-start(f32[768]{0:T(1024)} %get-tuple-element.1328) | copy-start | bytes 9220
  1733.8 67.5 %copy-start.128 = (f32[256]{0:T(256)S(1)}, f32[256]{0:T(256)}, u32[]{:S(2)}) copy-start(f32[256]{0:T(256)} %copy-done.127) | copy-start | bytes 3076
  1733.8 67.5 %copy-start.139 = (f32[256]{0:T(256)S(1)}, f32[256]{0:T(256)}, u32[]{:S(2)}) copy-start(f32[256]{0:T(256)} %copy-done.138) | copy-start | bytes 3076
  (323 other events, 2595.6 us)
Sparse Core Ops, SparseCore 0:
  12.4 22.3 all-gather.8
  236.4 28.1 reduce-scatter.8
  267.8 19.6 all-gather.10
  294.9 28.1 reduce-scatter.10
  325.5 19.6 all-gather.12
  699.6 28.1 reduce-scatter.12
  731.9 19.6 all-gather.14
  753.2 19.6 all-gather.16
  781.6 28.1 reduce-scatter.16
  815.1 19.6 all-gather.18
  1207.9 28.1 reduce-scatter.18
  1239.2 28.1 reduce-scatter.14
  1271.1 19.6 all-gather.20
  1298.4 28.1 reduce-scatter.20
  1331.7 19.6 all-gather.22
  1715.7 28.1 reduce-scatter.22
  1750.2 350.7 all-reduce.7
where the time goes:
time: 2150 us; the launch traced here: 2120 us
  other arithmetic  1020 us (47%)
  waiting for transfers between devices  608 us (28%)
  local copies, waits for them, and re-layouts  321 us (15%)
  matrix products  88 us (4%)
  blocking collectives  64.7 us (3%)
    reduce_sum x32, other arithmetic, retreat(): jnp.sum(weight_cos * piece_re[None] - weight_sin * piece_im[None], axis=1)  341 us
    reduce_sum x32, other arithmetic, advance(): jnp.sum(weight_cos * piece_im[None] + weight_sin * piece_re[None], axis=1)  324 us
    psum x1, waiting for transfers between devices, local(): lax.psum((stacked[0], stacked[1], stacked[2], stacked[3], stacked[4], sta...  297 us
    squeeze x64, local copies, waits for them, and re-layouts, forward_states(): final_state, states = lax.scan(advance, start_state, pieces_all)  66.1 us
    reduce_scatter x2, waiting for transfers between devices, local(): lax.psum_scatter((jnp.dot(mixed_re, out_re, preferred_element_type=jnp.fl...  56.5 us
    reduce_scatter x2, waiting for transfers between devices, local(): lax.psum_scatter(jnp.dot(hidden, down_mat, preferred_element_type=jnp.flo...  55.7 us
    all_gather x4, waiting for transfers between devices, local(): lax.all_gather(gradient.astype(jnp.bfloat16), 'tensor', axis=0, tiled=True)  54.1 us
    another operation x32, other arithmetic, retreat(): running = jnp.cumsum(log_keep, axis=0)  46 us
  transfers between devices with their start and end apart: 17, of which 16 were waited for; matrix products, arithmetic and copies ran while one was open for 3% of the time, Pallas kernels for 0%

commit v1 on v0

v1 whole, which is shorter than its diff:
```python
import functools
import types

import jax
import jax.numpy as jnp
from jax import lax
from jax.experimental import pallas as pl
from jax.experimental.pallas import tpu as pltpu
from jax.sharding import PartitionSpec as P

MESH = pl.DeviceIdType.MESH
F32 = jnp.float32
BF16 = jnp.bfloat16

GROUP_CH = 48
EPS_NORM = 1e-06
EPS_GROUP = 1e-05
LANES = 128
SEGS = 8
CHUNKS = 4
VMEM_BYTES = 63 * 1024 * 1024


def sigmoid(v):
    return 0.5 * jnp.tanh(0.5 * v) + 0.5


def mm(left, right):
    return jnp.dot(left, right, preferred_element_type=F32)


def mm_nt(left, right):
    return lax.dot_general(left, right, (((1,), (1,)), ((), ())), preferred_element_type=F32)


def mm_tn(left, right):
    return lax.dot_general(left, right, (((0,), (0,)), ((), ())), preferred_element_type=F32)


def loop(count, body):
    def step(index, carry):
        body(index)
        return carry

    lax.fori_loop(0, count, step, 0)


def iota(shape, dim):
    return lax.broadcasted_iota(jnp.int32, shape, dim)


def scratch_of(z):
    L, D, C, F, R, N = z.L, z.D, z.C, z.F, z.R, CHUNKS
    rows = (2, N, 2, R)
    own = (N, R)
    bufs = dict(
        wmix=((L, D, 5 * C), BF16),
        wout=((L, 2 * C, D), BF16),
        wffn=((L, D, 2 * F), BF16),
        par=((L, 8, C), F32),
        ngf=((L, 2, D), F32),
        gsum=((C, C), BF16),
        st=((L + 1, 2, *own, D), F32),
        mixfull=((L, *rows, D), BF16),
        ffnfull=((L, *rows, D), BF16),
        gfull=((L, 2, *rows, D), BF16),
        proj=((L, *rows, 5 * C), F32),
        state=((L, 2, 2, 2, SEGS + N * R, C), F32),
        unit=((L, 2, *rows, C), F32),
        inv=((L, *rows, C), F32),
        mixed=((L, *rows, 2 * C), BF16),
        gup=((L, *rows, 2 * F), BF16),
        hidden=((L, *rows, F), BF16),
        keep=((*rows, C), F32),
        drive=((2, *rows, C), F32),
        seg=((3, 2, 2, SEGS, C), F32),
        segk=((L, 2, 2, SEGS, C), F32),
        cur=((2, 2, 2, SEGS, C), F32),
        tot=((2, 2, R, C), F32),
        dgu=((*rows, 2 * F), BF16),
        dproj=((*rows, 5 * C), BF16),
        psc=((2, R, D), F32),
        xpart=((*own, D), F32),
        opart=((*own, D), F32),
        grad=((*own, D), F32),
        stage=((3, *own, D), BF16),
        land=((2, 3, *own, D), BF16),
        gacc=((L, 2, SEGS, D), F32),
        sacc=((L, 4, SEGS, C), F32),
    )
    sems = dict(
        ags=(4 * L, 3, N),
        agr=(4 * L, 3, N),
        rss=(4 * L, 3, N),
        rsr=(4 * L, 3, N),
        wsem=(L, 2),
    )
    names = list(bufs) + list(sems)
    shapes = [pltpu.VMEM(s, d) for s, d in bufs.values()]
    shapes += [pltpu.SemaphoreType.DMA(s) for s in sems.values()]
    return names, shapes


IN_NAMES = ("x", "ct", "ng", "inw", "fw", "gw", "ow", "ph", "bl", "gg", "ffw", "dw")
OUT_NAMES = ("out", "ig", "gffn", "gdown", "gmix", "gout", "small", "gains")


def mega(z, names, *refs):
    r = types.SimpleNamespace(**dict(zip(IN_NAMES + OUT_NAMES + tuple(names), refs)))
    L, D, C, F, R, N = z.L, z.D, z.C, z.F, z.R, CHUNKS
    ch = z.ch
    Q = R // SEGS
    dp = lax.axis_index("dp")
    me = lax.axis_index("tensor")
    core = lax.rem(me, 2)
    xi = me // 2
    other = 1 - xi
    sib = xi * 2 + 1 - core
    xnb = other * 2 + core

    barrier = pltpu.get_barrier_semaphore()
    for peer in (sib, xnb):
        pl.semaphore_signal(barrier, inc=1, device_id=(dp, peer), device_id_type=MESH)
    pl.semaphore_wait(barrier, 2)

    def remote(src, dst, send, recv, peer):
        return pltpu.make_async_remote_copy(
            src_ref=src,
            dst_ref=dst,
            send_sem=send,
            recv_sem=recv,
            device_id=(dp, peer),
            device_id_type=MESH,
        )

    def ag_copy(e, full, c, kind):
        chip = other if kind == 2 else xi
        peer = xnb if kind == 0 else sib
        ref = full.at[chip, c, core]
        return remote(ref, ref, r.ags.at[e, kind, c], r.agr.at[e, kind, c], peer)

    def ag_landing(e, full, c, kind):
        chip = xi if kind == 1 else other
        col = core if kind == 0 else 1 - core
        ref = full.at[chip, c, col]
        return remote(ref, ref, r.ags.at[e, kind, c], r.agr.at[e, kind, c], sib)

    def ag_start(e, full, c):
        ag_copy(e, full, c, 0).start()
        ag_copy(e, full, c, 1).start()

    def ag_take_x(e, full, c):
        ag_landing(e, full, c, 0).wait_recv()
        ag_copy(e, full, c, 2).start()

    def rs_copy(e, c, kind):
        side = 0 if z.single_side else None
        return remote(
            r.stage.at[kind, c],
            r.land.at[r_side(e), kind, c],
            r.rss.at[e, kind, c],
            r.rsr.at[e, kind, c],
            xnb if kind == 1 else sib,
        )

    def r_side(e):
        return e // (2 * L)

    def rs_other(e, c):
        r.stage[0, c] = r.psc[1 - core].astype(BF16)
        rs_copy(e, c, 0).start()
        r.xpart[c] = r.psc[core]

    def rs_pass(e, c):
        rs_copy(e, c, 0).wait_recv()
        r.stage[1, c] = (r.xpart[c] + r.land[r_side(e), 0, c].astype(F32)).astype(BF16)
        rs_copy(e, c, 1).start()

    def rs_own(e, c):
        r.stage[2, c] = r.psc[1 - core].astype(BF16)
        rs_copy(e, c, 2).start()
        r.opart[c] = r.psc[core]

    def rs_final(e, full, c):
        rs_copy(e, c, 2).wait_recv()
        rs_copy(e, c, 1).wait_recv()
        side = r_side(e)
        total = r.opart[c] + r.land[side, 2, c].astype(F32) + r.land[side, 1, c].astype(F32)
        for kind in range(3):
            rs_copy(e, c, kind).wait_send()
            ag_copy(e, full, c, kind).wait_send()
        return total

    def gather_loop(e, full, order, stage):
        def step(j):
            @pl.when(j < N)
            def _():
                ag_landing(e, full, order(j), 1).wait_recv()

            @pl.when((j >= N - 1) & (j < 2 * N - 1))
            def _():
                ag_take_x(e, full, order(j - N + 1))

            @pl.when(j >= N)
            def _():
                ag_landing(e, full, order(j - N), 2).wait_recv()

            stage(j)

        loop(2 * N, step)

    def chip_chunk(j, order, own_first):
        first = j < N
        chunk = order(jnp.where(first, j, j - N))
        if own_first:
            return jnp.where(first, xi, other), chunk
        return jnp.where(first, other, xi), chunk

    ascending = lambda j: j
    descending = lambda j: N - 1 - j

    def norm_rows(s):
        return lax.rsqrt(jnp.mean(s * s, axis=-1, keepdims=True) + EPS_NORM)

    def group_sum(v):
        high = v.astype(BF16)
        rest = (v - high.astype(F32)).astype(BF16)
        weight = r.gsum[...]
        return (mm(high, weight) + mm(rest, weight)) * (1.0 / (2 * GROUP_CH))

    def fold(v):
        return jnp.sum(v.reshape(v.shape[0] // SEGS, SEGS, v.shape[1]), axis=0)

    def flat(v):
        return v.reshape(-1, v.shape[-1])

    w_copies = [
        pltpu.make_async_copy(
            r.ffw.at[l, k], r.wffn.at[l, :, pl.ds(k * F, F)], r.wsem.at[l, k]
        )
        for l in range(L)
        for k in range(2)
    ]
    for copy in w_copies:
        copy.start()

    tokens = N * R
    width = tokens // SEGS
    row = iota((tokens, tokens), 0)
    col = iota((tokens, tokens), 1)
    place = lax.rem(row, SEGS) * width + row // SEGS
    perm = jnp.where(col == place, 1.0, 0.0).astype(BF16)
    r.st[0, 0] = mm(perm, r.x[...]).reshape(N, R, D)
    r.grad[...] = mm(perm, r.ct[...]).reshape(N, R, D)

    r.ngf[...] = r.ng[...].astype(F32)
    r.wmix[...] = jnp.zeros_like(r.wmix)
    r.wout[...] = jnp.zeros_like(r.wout)
    r.par[...] = jnp.zeros_like(r.par)
    r.gacc[...] = jnp.zeros_like(r.gacc)
    r.sacc[...] = jnp.zeros_like(r.sacc)
    for l in range(L):
        parts = (r.inw.at[l, 0], r.inw.at[l, 1], r.fw.at[l], r.gw.at[l, 0], r.gw.at[l, 1])
        for k, part in enumerate(parts):
            r.wmix[l, :, k * C : k * C + ch] = part[...]
        for k in range(2):
            r.wout[l, k * C : k * C + ch, :] = r.ow[l, k]
        angle = r.ph[l : l + 1, :]
        turn_cos, turn_sin = jnp.cos(angle), jnp.sin(angle)
        r.par[l, 0:1, 0:ch] = turn_cos
        r.par[l, 1:2, 0:ch] = turn_sin
        r.par[l, 2:3, 0:ch] = sigmoid(r.bl[l : l + 1, :])
        r.par[l, 3:4, 0:ch] = r.gg[l, 0:1, :].astype(F32)
        r.par[l, 4:5, 0:ch] = r.gg[l, 1:2, :].astype(F32)
        for _ in range(width.bit_length() - 1):
            turn_cos, turn_sin = (
                turn_cos * turn_cos - turn_sin * turn_sin,
                2.0 * turn_cos * turn_sin,
            )
        r.par[l, 5:6, 0:ch] = turn_cos
        r.par[l, 6:7, 0:ch] = turn_sin
    gi, gj = iota((C, C), 0), iota((C, C), 1)
    same = (gi // GROUP_CH == gj // GROUP_CH) & (gi < ch) & (gj < ch)
    r.gsum[...] = jnp.where(same, 1.0, 0.0).astype(BF16)

    def rows_of(q):
        return slice(q * SEGS, (q + 1) * SEGS)

    def scan_local(l, chip, c, turn_cos, turn_sin):
        for k in range(2):
            h_re, h_im, prod = r.seg[0, chip, k], r.seg[1, chip, k], r.seg[2, chip, k]
            for q in range(Q):
                rate = r.keep[chip, c, k, rows_of(q), :]
                h_re, h_im = (
                    rate * (turn_cos * h_re - turn_sin * h_im) + r.drive[0, chip, c, k, rows_of(q), :],
                    rate * (turn_cos * h_im + turn_sin * h_re) + r.drive[1, chip, c, k, rows_of(q), :],
                )
                prod = prod * rate
            r.seg[0, chip, k], r.seg[1, chip, k], r.seg[2, chip, k] = h_re, h_im, prod

    def scan_final(l, chip, c, turn_cos, turn_sin):
        base = SEGS + c * R
        for k in range(2):
            h_re, h_im = r.cur[0, chip, k], r.cur[1, chip, k]
            for q in range(Q):
                rate = r.keep[chip, c, k, rows_of(q), :]
                h_re, h_im = (
                    rate * (turn_cos * h_re - turn_sin * h_im) + r.drive[0, chip, c, k, rows_of(q), :],
                    rate * (turn_cos * h_im + turn_sin * h_re) + r.drive[1, chip, c, k, rows_of(q), :],
                )
                at = pl.ds(pl.multiple_of(base + q * SEGS, SEGS), SEGS)
                r.state[l, 0, chip, k, at, :] = h_re
                r.state[l, 1, chip, k, at, :] = h_im
            r.cur[0, chip, k], r.cur[1, chip, k] = h_re, h_im

    def scan_back_local(l, chip, c, turn_cos, turn_sin):
        for k in range(2):
            u_re, u_im = r.seg[0, chip, k], r.seg[1, chip, k]
            for q in reversed(range(Q)):
                rate = r.keep[chip, c, k, rows_of(q), :]
                t_re = r.drive[0, chip, c, k, rows_of(q), :] + u_re
                t_im = r.drive[1, chip, c, k, rows_of(q), :] + u_im
                u_re = rate * (turn_cos * t_re + turn_sin * t_im)
                u_im = rate * (turn_cos * t_im - turn_sin * t_re)
            r.seg[0, chip, k], r.seg[1, chip, k] = u_re, u_im

    def scan_back_final(l, chip, c, turn_cos, turn_sin):
        for k in range(2):
            u_re, u_im = r.cur[0, chip, k], r.cur[1, chip, k]
            for q in reversed(range(Q)):
                rate = r.keep[chip, c, k, rows_of(q), :]
                t_re = r.drive[0, chip, c, k, rows_of(q), :] + u_re
                t_im = r.drive[1, chip, c, k, rows_of(q), :] + u_im
                r.tot[0, k, rows_of(q), :] = t_re
                r.tot[1, k, rows_of(q), :] = t_im
                u_re = rate * (turn_cos * t_re + turn_sin * t_im)
                u_im = rate * (turn_cos * t_im - turn_sin * t_re)
            r.cur[0, chip, k], r.cur[1, chip, k] = u_re, u_im

    def carry_over(l, back):
        all_cos, all_sin = r.par[l, 5:6, :], r.par[l, 6:7, :]
        if back:
            all_sin = -all_sin
        c_re = jnp.zeros((1, C), F32)
        c_im = jnp.zeros((1, C), F32)
        order = [(chip, k, s) for chip in range(2) for k in range(2) for s in range(SEGS)]
        for chip, k, s in reversed(order) if back else order:
            one = slice(s, s + 1)
            r.cur[0, chip, k, one, :] = c_re
            r.cur[1, chip, k, one, :] = c_im
            prod = r.segk[l, chip, k, one, :]
            c_re, c_im = (
                prod * (all_cos * c_re - all_sin * c_im) + r.seg[0, chip, k, one, :],
                prod * (all_cos * c_im + all_sin * c_re) + r.seg[1, chip, k, one, :],
            )

    def forward_layer(l):
        turn_cos, turn_sin, lower = r.par[l, 0:1, :], r.par[l, 1:2, :], r.par[l, 2:3, :]
        gain_re, gain_im = r.par[l, 3:4, :], r.par[l, 4:5, :]
        e = 2 * l
        full = r.mixfull.at[l]

        def send_mix(c):
            @pl.when(l > 0)
            def _():
                r.st[l, 0, c] = r.st[l - 1, 1, c] + rs_final(e - 1, r.ffnfull.at[l - 1], c)

            s = r.st[l, 0, c]
            full[xi, c, core] = (s * norm_rows(s) * r.ngf[l, 0:1, :]).astype(BF16)
            ag_start(e, full, c)

        loop(N, send_mix)

        r.seg[0:2] = jnp.zeros((2, 2, 2, SEGS, C), F32)
        r.seg[2] = jnp.ones((2, 2, SEGS, C), F32)

        def project(j):
            chip, c = chip_chunk(j, ascending, True)
            proj = mm(flat(full[chip, c]), r.wmix[l])
            r.proj[l, chip, c] = proj.reshape(2, R, 5 * C)
            in_re, in_im, pre = proj[:, 0:C], proj[:, C : 2 * C], proj[:, 2 * C : 3 * C]
            rate = lower + (1.0 - lower) * sigmoid(pre)
            r.keep[chip, c] = rate.reshape(2, R, C)
            r.drive[0, chip, c] = ((1.0 - rate) * in_re * sigmoid(in_re)).reshape(2, R, C)
            r.drive[1, chip, c] = ((1.0 - rate) * in_im * sigmoid(in_im)).reshape(2, R, C)
            scan_local(l, chip, c, turn_cos, turn_sin)

        gather_loop(e, full, ascending, project)
        r.segk[l] = r.seg[2]
        carry_over(l, False)
        for part in range(2):
            r.state[l, part, :, :, 0:SEGS, :] = r.cur[part]

        def mix(j):
            chip, c = chip_chunk(j, ascending, False)
            scan_final(l, chip, c, turn_cos, turn_sin)
            at = pl.ds(pl.multiple_of(SEGS + c * R, SEGS), R)
            s_re = flat(r.state[l, 0, chip, :, at, :])
            s_im = flat(r.state[l, 1, chip, :, at, :])
            centre = group_sum(s_re + s_im)
            d_re, d_im = s_re - centre, s_im - centre
            scale = lax.rsqrt(group_sum(d_re * d_re + d_im * d_im) + EPS_GROUP)
            u_re, u_im = d_re * scale, d_im * scale
            r.unit[l, 0, chip, c] = u_re.reshape(2, R, C)
            r.unit[l, 1, chip, c] = u_im.reshape(2, R, C)
            r.inv[l, chip, c] = scale.reshape(2, R, C)
            gate_re = flat(r.proj[l, chip, c, :, :, 3 * C : 4 * C])
            gate_im = flat(r.proj[l, chip, c, :, :, 4 * C : 5 * C])
            m_re = (u_re * gain_re * sigmoid(gate_re)).astype(BF16)
            m_im = (u_im * gain_im * sigmoid(gate_im)).astype(BF16)
            r.mixed[l, chip, c, :, :, 0:C] = m_re.reshape(2, R, C)
            r.mixed[l, chip, c, :, :, C : 2 * C] = m_im.reshape(2, R, C)
            r.psc[...] = mm(flat(r.mixed[l, chip, c]), r.wout[l]).reshape(2, R, D)

            @pl.when(j < N)
            def _():
                rs_other(e, c)

            @pl.when((j >= 1) & (j <= N))
            def _():
                rs_pass(e, j - 1)

            @pl.when(j >= N)
            def _():
                rs_own(e, c)

        loop(2 * N, mix)

        e2 = e + 1
        full2 = r.ffnfull.at[l]

        def send_ffn(c):
            s = r.st[l, 0, c] + rs_final(e, full, c)
            r.st[l, 1, c] = s
            full2[xi, c, core] = (s * norm_rows(s) * r.ngf[l, 1:2, :]).astype(BF16)
            ag_start(e2, full2, c)

        loop(N, send_ffn)

        @pl.when(l == 0)
        def _():
            for copy in w_copies:
                copy.wait()

        def feed(j):
            chip, c = chip_chunk(j, ascending, True)
            both = mm(flat(full2[chip, c]), r.wffn[l])
            r.gup[l, chip, c] = both.astype(BF16).reshape(2, R, 2 * F)
            gate, up = both[:, 0:F], both[:, F : 2 * F]
            hidden = (gate * sigmoid(gate) * up).astype(BF16)
            r.hidden[l, chip, c] = hidden.reshape(2, R, F)
            r.psc[...] = mm(hidden, r.dw[l]).reshape(2, R, D)

            @pl.when(j < N)
            def _():
                rs_own(e2, c)

            @pl.when(j >= N)
            def _():
                rs_other(e2, c)

            @pl.when(j > N)
            def _():
                rs_pass(e2, j - N - 1)

        gather_loop(e2, full2, ascending, feed)
        rs_pass(e2, N - 1)

    loop(L, forward_layer)

    def last_sum(c):
        e = 2 * L - 1
        r.st[L, 0, c] = r.st[L - 1, 1, c] + rs_final(e, r.ffnfull.at[L - 1], c)

    loop(N, last_sum)
    unperm = perm
    r.out[...] = mm_tn(unperm, r.st[L, 0].reshape(tokens, D).astype(BF16)).astype(BF16)

    def norm_back(l, which, c, grad_out):
        s = r.st[l, which, c]
        scale = norm_rows(s)
        r.gacc[l, which] += fold(grad_out * s * scale)
        scaled = grad_out * r.ngf[l, which : which + 1, :]
        back = scale * scaled - s * (scale * scale * scale) * jnp.mean(
            scaled * s, axis=-1, keepdims=True
        )
        r.grad[c] = r.grad[c] + back

    def backward_layer(step):
        l = L - 1 - step
        e = 2 * L + 2 * step
        full = r.gfull.at[l, 0]

        def send_ffn(j):
            c = descending(j)

            @pl.when(step > 0)
            def _():
                norm_back(l + 1, 0, c, rs_final(e - 1, r.gfull.at[l + 1, 1], c))

            full[xi, c, core] = r.grad[c].astype(BF16)
            ag_start(e, full, c)

        loop(N, send_ffn)

        def feed_back(j):
            chip, c = chip_chunk(j, descending, True)
            g_hidden = mm_nt(flat(full[chip, c]), r.dw[l])
            both = flat(r.gup[l, chip, c]).astype(F32)
            gate, up = both[:, 0:F], both[:, F : 2 * F]
            s = sigmoid(gate)
            g_gate = (g_hidden * up * s * (1.0 + gate * (1.0 - s))).astype(BF16)
            g_up = (g_hidden * gate * s).astype(BF16)
            r.dgu[chip, c, :, :, 0:F] = g_gate.reshape(2, R, F)
            r.dgu[chip, c, :, :, F : 2 * F] = g_up.reshape(2, R, F)
            r.psc[...] = mm_nt(flat(r.dgu[chip, c]), r.wffn[l]).reshape(2, R, D)

            @pl.when(j < N)
            def _():
                rs_own(e, c)

            @pl.when(j >= N)
            def _():
                rs_other(e, c)

            @pl.when(j > N)
            def _():
                rs_pass(e, descending(j - N - 1))

        gather_loop(e, full, descending, feed_back)
        rs_pass(e, 0)

        def down_tile(i):
            cols = pl.ds(pl.multiple_of(i * LANES, LANES), LANES)
            r.gdown[l, cols, :] = mm_tn(flat(r.hidden[l, :, :, :, :, cols]), flat(full[...])).astype(BF16)

        loop(F // LANES, down_tile)

        def ffn_tile(i):
            cols = pl.ds(pl.multiple_of(i * LANES, LANES), LANES)
            r.gffn[l, cols, :] = mm_tn(flat(r.ffnfull[l, :, :, :, :, cols]), flat(r.dgu[...])).astype(BF16)

        loop(D // LANES, ffn_tile)

        turn_cos, turn_sin, lower = r.par[l, 0:1, :], r.par[l, 1:2, :], r.par[l, 2:3, :]
        gain_re, gain_im = r.par[l, 3:4, :], r.par[l, 4:5, :]
        e2 = e + 1
        full2 = r.gfull.at[l, 1]

        def send_mix(j):
            c = descending(j)
            norm_back(l, 1, c, rs_final(e, full, c))
            full2[xi, c, core] = r.grad[c].astype(BF16)
            ag_start(e2, full2, c)

        loop(N, send_mix)
        r.seg[0:2] = jnp.zeros((2, 2, 2, SEGS, C), F32)

        def mix_back(j):
            chip, c = chip_chunk(j, descending, True)
            g_both = mm_nt(flat(full2[chip, c]), r.wout[l])
            g_re, g_im = g_both[:, 0:C], g_both[:, C : 2 * C]
            s_re = sigmoid(flat(r.proj[l, chip, c, :, :, 3 * C : 4 * C]))
            s_im = sigmoid(flat(r.proj[l, chip, c, :, :, 4 * C : 5 * C]))
            u_re, u_im = flat(r.unit[l, 0, chip, c]), flat(r.unit[l, 1, chip, c])
            n_re, n_im = g_re * s_re, g_im * s_im
            r.sacc[l, 0] += fold(n_re * u_re)
            r.sacc[l, 1] += fold(n_im * u_im)
            x_re, x_im = n_re * gain_re, n_im * gain_im
            cross_re, cross_im = x_re * u_re, x_im * u_im
            r.dproj[chip, c, :, :, 3 * C : 4 * C] = (cross_re * (1.0 - s_re)).astype(BF16).reshape(2, R, C)
            r.dproj[chip, c, :, :, 4 * C : 5 * C] = (cross_im * (1.0 - s_im)).astype(BF16).reshape(2, R, C)
            mean_one = group_sum(x_re + x_im)
            mean_two = group_sum(cross_re + cross_im)
            scale = flat(r.inv[l, chip, c])
            r.drive[0, chip, c] = (scale * (x_re - mean_one - u_re * mean_two)).reshape(2, R, C)
            r.drive[1, chip, c] = (scale * (x_im - mean_one - u_im * mean_two)).reshape(2, R, C)
            pre = flat(r.proj[l, chip, c, :, :, 2 * C : 3 * C])
            r.keep[chip, c] = (lower + (1.0 - lower) * sigmoid(pre)).reshape(2, R, C)
            scan_back_local(l, chip, c, turn_cos, turn_sin)

        gather_loop(e2, full2, descending, mix_back)
        carry_over(l, True)

        def scan_back(j):
            chip, c = chip_chunk(j, descending, False)
            scan_back_final(l, chip, c, turn_cos, turn_sin)
            t_re, t_im = flat(r.tot[0]), flat(r.tot[1])
            at = pl.ds(pl.multiple_of(c * R, SEGS), R)
            p_re = flat(r.state[l, 0, chip, :, at, :])
            p_im = flat(r.state[l, 1, chip, :, at, :])
            in_re = flat(r.proj[l, chip, c, :, :, 0:C])
            in_im = flat(r.proj[l, chip, c, :, :, C : 2 * C])
            fs = sigmoid(flat(r.proj[l, chip, c, :, :, 2 * C : 3 * C]))
            rate = lower + (1.0 - lower) * fs
            s_re, s_im = sigmoid(in_re), sigmoid(in_im)
            gc_re = t_re * p_re + t_im * p_im
            gc_im = t_im * p_re - t_re * p_im
            g_keep = gc_re * turn_cos + gc_im * turn_sin - (t_re * in_re * s_re + t_im * in_im * s_im)
            r.sacc[l, 2] += fold(rate * (gc_im * turn_cos - gc_re * turn_sin))
            r.sacc[l, 3] += fold(g_keep * (1.0 - fs))
            d_re = t_re * (1.0 - rate) * s_re * (1.0 + in_re * (1.0 - s_re))
            d_im = t_im * (1.0 - rate) * s_im * (1.0 + in_im * (1.0 - s_im))
            d_f = g_keep * (1.0 - lower) * fs * (1.0 - fs)
            r.dproj[chip, c, :, :, 0:C] = d_re.astype(BF16).reshape(2, R, C)
            r.dproj[chip, c, :, :, C : 2 * C] = d_im.astype(BF16).reshape(2, R, C)
            r.dproj[chip, c, :, :, 2 * C : 3 * C] = d_f.astype(BF16).reshape(2, R, C)
            r.psc[...] = mm_nt(flat(r.dproj[chip, c]), r.wmix[l]).reshape(2, R, D)

            @pl.when(j < N)
            def _():
                rs_other(e2, c)

            @pl.when((j >= 1) & (j <= N))
            def _():
                rs_pass(e2, descending(j - 1))

            @pl.when(j >= N)
            def _():
                rs_own(e2, c)

        loop(2 * N, scan_back)

        def out_tile(i):
            cols = pl.ds(pl.multiple_of(i * LANES, LANES), LANES)
            r.gout[l, cols, :] = mm_tn(flat(r.mixed[l, :, :, :, :, cols]), flat(full2[...])).astype(BF16)

        loop(2 * C // LANES, out_tile)

        def mix_tile(i):
            cols = pl.ds(pl.multiple_of(i * LANES, LANES), LANES)
            r.gmix[l, cols, :] = mm_tn(flat(r.mixfull[l, :, :, :, :, cols]), flat(r.dproj[...])).astype(BF16)

        loop(D // LANES, mix_tile)

    loop(L, backward_layer)

    def last_grad(j):
        c = descending(j)
        norm_back(0, 0, c, rs_final(4 * L - 1, r.gfull.at[0, 1], c))

    loop(N, last_grad)
    r.ig[...] = mm_tn(perm, r.grad[...].reshape(tokens, D).astype(BF16)).astype(BF16)
    for l in range(L):
        for which in range(2):
            r.gains[2 * l + which : 2 * l + which + 1, :] = jnp.sum(r.gacc[l, which], axis=0, keepdims=True)
        for k in range(4):
            value = jnp.sum(r.sacc[l, k], axis=0, keepdims=True)
            if k == 3:
                lower = r.par[l, 2:3, :]
                value = value * lower * (1.0 - lower)
            r.small[4 * l + k : 4 * l + k + 1, :] = value


def local(*args):
    x, ct, ng, inw, fw, gw, ow, ph, bl, gg, ffw, dw = args
    L, D = ng.shape[0], ng.shape[2]
    ch = fw.shape[2]
    F = dw.shape[1]
    C = -(-ch // LANES) * LANES
    z = types.SimpleNamespace(L=L, D=D, C=C, F=F, ch=ch, R=x.shape[0] // CHUNKS, single_side=False)
    names, scratch = scratch_of(z)
    vmem = pl.BlockSpec(memory_space=pltpu.VMEM)
    in_specs = [vmem] * 12
    in_specs[10] = pl.BlockSpec(memory_space=pl.ANY)
    shape = jax.ShapeDtypeStruct
    out, ig, gffn, gdown, gmix, gout, small, gains = pl.pallas_call(
        functools.partial(mega, z, names),
        out_shape=(
            shape(x.shape, BF16),
            shape(x.shape, BF16),
            shape((L, D, 2 * F), BF16),
            shape((L, F, D), BF16),
            shape((L, D, 5 * C), BF16),
            shape((L, 2 * C, D), BF16),
            shape((4 * L, C), F32),
            shape((2 * L, D), F32),
        ),
        in_specs=in_specs,
        out_specs=[vmem] * 8,
        scratch_shapes=scratch,
        compiler_params=pltpu.CompilerParams(
            collective_id=0, has_side_effects=True, vmem_limit_bytes=VMEM_BYTES
        ),
        name="layers",
    )(x, ct, ng, inw, fw, gw, ow, ph, bl, gg, ffw, dw)

    gffn, gdown, gmix, gout, small = lax.psum((gffn, gdown, gmix, gout, small), "dp")
    gains = lax.psum(gains, ("dp", "tensor")).reshape(L, 2, D)
    piece = D // lax.axis_size("tensor")
    gains = lax.dynamic_slice_in_dim(gains, lax.axis_index("tensor") * piece, piece, 2)
    gmix = gmix.astype(F32).reshape(L, D, 5, C)[..., :ch]
    small = small.reshape(L, 4, C)[..., :ch]
    return (
        out,
        ig,
        gains,
        jnp.stack([gmix[:, :, 0], gmix[:, :, 1]], axis=1),
        gmix[:, :, 2],
        jnp.stack([gmix[:, :, 3], gmix[:, :, 4]], axis=1),
        gout.astype(F32).reshape(L, 2, C, D)[:, :, :ch],
        small[:, 2],
        small[:, 3],
        small[:, 0:2],
        jnp.stack([gffn[:, :, :F], gffn[:, :, F:]], axis=1).astype(F32),
        gdown.astype(F32),
    )


def solution(mesh):
    tokens = P(("dp", "tensor"), None)
    return jax.shard_map(
        local,
        mesh=mesh,
        in_specs=(
            tokens,
            tokens,
            P(),
            P(None, None, None, "tensor"),
            P(None, None, "tensor"),
            P(None, None, None, "tensor"),
            P(None, None, "tensor", None),
            P(None, "tensor"),
            P(None, "tensor"),
            P(None, None, "tensor"),
            P(None, None, None, "tensor"),
            P(None, "tensor", None),
        ),
        out_specs=(
            tokens,
            tokens,
            P(None, None, "tensor"),
            P(None, None, None, "tensor"),
            P(None, None, "tensor"),
            P(None, None, None, "tensor"),
            P(None, None, "tensor", None),
            P(None, "tensor"),
            P(None, "tensor"),
            P(None, None, "tensor"),
            P(None, None, None, "tensor"),
            P(None, "tensor", None),
        ),
        check_vma=False,
    )
```

time: 2150 us -> 427 us (0.20); the launches traced: 2120 us -> 427 us
  other arithmetic: 1020 us -> 5.04 us
  waiting for transfers between devices: 608 us -> 152 us
  local copies, waits for them, and re-layouts: 321 us -> 19.3 us
  Pallas kernels: 0 us -> 174 us
  matrix products: 88 us -> 0 us
    reduce_sum x82 -> x0, other arithmetic: 696 us -> none  [the longest x32 341 us: retreat(): jnp.sum(weight_cos * piece_re[None] - weight_sin * piece_im[None], axis=1)]
    reduce_scatter x8 -> x0, waiting for transfers between devices: 181 us -> none  [the longest x2 56.5 us: local(): lax.psum_scatter((jnp.dot(mixed_re, out_re, preferred_element_type=jnp.fl...]
    pallas_call x0 -> x1, Pallas kernels: none -> 174 us  [local(): pl.pallas_call(functools.partial(mega, z, names), out_shape=(shape(x.shap...]
    psum x1, waiting for transfers between devices: 297 us -> 152 us  [local(): lax.psum((gffn, gdown, gmix, gout, small), 'dp')]
    all_gather x8 -> x0, waiting for transfers between devices: 129 us -> none  [the longest x4 54.1 us: local(): lax.all_gather(gradient.astype(jnp.bfloat16), 'tensor', axis=0, tiled=True)]
    mul x68 -> x0, other arithmetic: 88.6 us -> none  [the longest x32 39.9 us: retreat(): next_im = first_keep * (step_cos * total_im[0] - step_sin * total_re[0])]
    dot_general x54 -> x0, matrix products: 88 us -> none  [the longest x18 34.2 us: contract_cols(): lax.dot_general(left, right, (((1,), (1,)), ((), ())), preferred_element_...]
    another operation x83 -> x1, other arithmetic: 82.6 us -> 0.15 us  [local(): jnp.stack([gmix[:, :, 0], gmix[:, :, 1]], axis=1)]
  transfers between devices with their start and end apart: 17 -> 1, of which waited for: 16 -> 1; matrix products, arithmetic and copies ran while one was open for 3% -> 0% of each run, Pallas kernels for 0% -> 0%
where the time goes in v1:
time: 427 us
  Pallas kernels  174 us (41%)
  waiting for transfers between devices  152 us (36%)
  blocking collectives  62.1 us (15%)
  local copies, waits for them, and re-layouts  19.3 us (5%)
  between operations  14.1 us (3%)
  other arithmetic  5.04 us (1%)
    pallas_call x1, Pallas kernels, local(): pl.pallas_call(functools.partial(mega, z, names), out_shape=(shape(x.shap...  174 us
    psum x1, waiting for transfers between devices, local(): lax.psum((gffn, gdown, gmix, gout, small), 'dp')  152 us
    psum x1, blocking collectives, local(): gains = lax.psum(gains, ('dp', 'tensor')).reshape(L, 2, D)  39.8 us
    psum x1, blocking collectives, local(): lax.psum((gffn, gdown, gmix, gout, small), 'dp')  22.3 us
    unnamed x26, local copies, waits for them, and re-layouts  12.2 us
  transfers between devices with their start and end apart: 1, of which 1 were waited for; matrix products, arithmetic and copies ran while one was open for 0% of the time, Pallas kernels for 0%

profile of v1, /device:TPU:0, one launch (start us, length us, event | category | flops | bytes accessed | tf_op | source)
XLA Modules:
  0.0 427.0 jit_solution(10336249635863543815)
XLA Ops:
  7.2 0.0 copy-start.2
  7.2 0.0 copy-start.6
  7.2 0.0 all-reduce.3.cloned.1.call-start
  7.2 2.3 copy.31.refs_3_
  9.5 0.0 copy-done.2
  9.5 1.2 copy.33.refs_5_
  10.7 0.0 copy-done.6
  10.7 0.9 copy.32.refs_4_
  11.6 174.5 %layers.1 = (bf16[256,768]{1,0:T(8,128)(2,1)}, bf16[256,768]{1,0:T(8,128)(2,1)}, bf16[2,768,768]{2,1,0:T(8,128)(2,1)}, bf16[2,384,768]{2,1,0:T(8,128)(2,1)}, bf1...) custom-call(bf16[256,768]{1,0:T(8,128)(2,1)} %refs_0_.1, ...), custom_call_target="tpu_custom_call" | custom-call | tf_op jit(solution)/shard_map/layers/pallas_call | solution.py:667
  186.1 4.0 copy.34
  190.1 0.0 copy-start.7
  190.1 0.0 copy-start.8
  190.1 0.0 all-reduce.3.cloned.1.call-update
  190.1 0.7 copy-done.7
  190.8 0.0 copy-done.8
  190.8 22.3 %psum.45 = f32[2,4,128]{2,1,0:T(4,128)S(1)} all-reduce(f32[2,4,128]{2,1,0:T(4,128)S(1)} %bitcast.25), channel_id=1, replica_groups=mesh['dp'=8,'tensor'=4] {'dp'}, use_global_device_ids=true, to_apply=%region_3.0 | all-reduce | flops 1024 | bytes 8192 | tf_op jit(solution)/shard_map/psum | solution.py:688
  213.1 0.6 slice.66
  213.7 39.8 %psum.42 = f32[2,2,768]{2,1,0:T(2,128)S(1)} all-reduce(f32[2,2,768]{2,1,0:T(2,128)S(1)} %reshape.40), channel_id=1, replica_groups=mesh['dp'=8,'tensor'=4] {'dp','tensor'}, use_global_device_ids=true, to_apply=%region_0.0 | all-reduce | flops 3072 | bytes 24576 | tf_op jit(solution)/shard_map/psum | solution.py:689
  253.5 0.7 constant_dynamic-slice_fusion
  254.2 0.6 fusion
  254.8 151.8 %all-reduce.3.cloned.1.call-done = (bf16[2,768,5,128]{1,3,2,0:T(8,128)(2,1)}, bf16[2,2,128,768]{3,2,1,0:T(8,128)(2,1)}, bf16[2,768,768]{2,1,0:T(8,128)(2,1)}, bf16[2,384,768]{2,1,0:T(8,128)(2,1)}) async-done(((bf16[2,768,5,128]{1,3,2,0:T(8,128)(2,1)}, bf16[2,2,128,768]{3,2,1,0:T(8,128)(2,1)}, bf16[2,768,768]{2,1,0:T(8,128)(2,1)}, bf16[2,384,768]{2,1,0:T(8,128)(2,1)}), (bf16[2,768,5,128]{1,3,2,0:T(8,128)(2,1)}, ...) | async-done | bytes 6291472 | tf_op jit(solution)/shard_map/psum | solution.py:688
  406.6 1.9 reshape.42
  408.5 1.1 slice_bitcast_fusion.3
  409.6 0.2 pad_maximum_fusion
  409.7 1.1 copy.37
  410.8 0.0 copy-start
  410.8 1.1 copy.38
  411.9 1.0 copy-done
  412.9 0.2 slice_bitcast_fusion.1
  413.2 0.3 maximum_convert_fusion
  413.5 0.0 copy-start.1
  413.5 2.5 copy.39
  416.0 0.0 copy-done.1
  416.0 0.0 copy-start.3
  416.0 1.6 convert_element_type.9
  417.6 0.0 copy-start.5
  417.6 0.0 copy-done.3
  417.6 0.0 copy-start.4
  417.6 1.1 slice_convert_fusion
  418.7 0.0 copy-done.5
  418.7 0.7 copy.48
  419.4 0.0 copy-done.4
  419.4 0.7 copy.49
  (1 shorter events, 0.0 us)
Async XLA Ops:
  7.2 2.4 copy-start.2
  7.2 3.5 copy-start.6
  7.2 399.4 %all-reduce.3.cloned.1.call-start = ((), (), s32[]{:S(2)}) async-start(), calls=%async_computation | async-start | bytes 12582912 | tf_op jit(solution)/shard_map/psum | solution.py:688
  190.1 0.7 copy-start.7
  190.1 0.7 copy-start.8
  410.8 2.1 copy-start
  413.5 2.5 copy-start.1
  416.0 1.6 copy-start.3
  417.6 1.1 copy-start.5
  417.6 1.9 copy-start.4
Sparse Core Ops, SparseCore 0:
  190.2 216.3 all-reduce.2

commit v2 on v1

--- a/solution.py
+++ b/solution.py
@@ -54,16 +54,16 @@
     rows = (2, N, 2, R)
     own = (N, R)
     bufs = dict(
-        wmix=((L, D, 5 * C), BF16),
+        wmix=((L, 5 * C, D), BF16),
         wout=((L, 2 * C, D), BF16),
         wffn=((L, D, 2 * F), BF16),
         par=((L, 8, C), F32),
         ngf=((L, 2, D), F32),
         gsum=((C, C), BF16),
-        st=((L + 1, 2, *own, D), F32),
+        st=((2 * L + 1, *own, D), F32),
         mixfull=((L, *rows, D), BF16),
         ffnfull=((L, *rows, D), BF16),
-        gfull=((L, 2, *rows, D), BF16),
+        gfull=((2, *rows, D), BF16),
         proj=((L, *rows, 5 * C), F32),
         state=((L, 2, 2, 2, SEGS + N * R, C), F32),
         unit=((L, 2, *rows, C), F32),
@@ -87,22 +87,34 @@
         land=((2, 3, *own, D), BF16),
         gacc=((L, 2, SEGS, D), F32),
         sacc=((L, 4, SEGS, C), F32),
+        wdown=((L, F, D), BF16),
+        swork=((2 * SEGS, D), F32),
+        sland=((5, 2 * SEGS, D), F32),
     )
+    if z.reduce:
+        unit = (z.units * L, z.blk, D)
+        bufs.update(yland=(unit, BF16), zland=(unit, BF16), mland=(unit, BF16))
     sems = dict(
         ags=(4 * L, 3, N),
         agr=(4 * L, 3, N),
         rss=(4 * L, 3, N),
         rsr=(4 * L, 3, N),
-        wsem=(L, 2),
+        wsem=(L, 10),
+        ss=(5,),
+        sr=(5,),
     )
+    if z.reduce:
+        sems.update(us=(z.units * L, 5), ur=(z.units * L, 5))
     names = list(bufs) + list(sems)
     shapes = [pltpu.VMEM(s, d) for s, d in bufs.values()]
     shapes += [pltpu.SemaphoreType.DMA(s) for s in sems.values()]
+    names.append("freed")
+    shapes.append(pltpu.SemaphoreType.REGULAR)
     return names, shapes
 
 
 IN_NAMES = ("x", "ct", "ng", "inw", "fw", "gw", "ow", "ph", "bl", "gg", "ffw", "dw")
-OUT_NAMES = ("out", "ig", "gffn", "gdown", "gmix", "gout", "small", "gains")
+OUT_NAMES = ("out", "ig", "wg", "sums")
 
 
 def mega(z, names, *refs):
@@ -118,10 +130,26 @@
     sib = xi * 2 + 1 - core
     xnb = other * 2 + core
 
+    inner = lax.rem(dp, 8)
+    base = dp - inner
+    y = lax.rem(inner, 2)
+    line = inner // 2
+    middle = (line == 1) | (line == 2)
+
+    def on_line(place, row):
+        return (base + 2 * place + row, me)
+
+    y_peer = on_line(line, 1 - y)
+    pair_peer = on_line(line + 1 - 2 * lax.rem(line, 2), y)
+    cross_peer = on_line(3 - line, y)
+
+    peers = [(dp, sib), (dp, xnb)]
+    if z.reduce:
+        peers += [y_peer, pair_peer, cross_peer]
     barrier = pltpu.get_barrier_semaphore()
-    for peer in (sib, xnb):
-        pl.semaphore_signal(barrier, inc=1, device_id=(dp, peer), device_id_type=MESH)
-    pl.semaphore_wait(barrier, 2)
+    for peer in peers:
+        pl.semaphore_signal(barrier, inc=1, device_id=peer, device_id_type=MESH)
+    pl.semaphore_wait(barrier, len(peers))
 
     def remote(src, dst, send, recv, peer):
         return pltpu.make_async_remote_copy(
@@ -129,9 +157,89 @@
             dst_ref=dst,
             send_sem=send,
             recv_sem=recv,
-            device_id=(dp, peer),
+            device_id=peer if isinstance(peer, tuple) else (dp, peer),
             device_id_type=MESH,
         )
+
+    def unit_of(u):
+        return L - 1 - u // z.units, lax.rem(u, z.units)
+
+    def unit_copy(u, stage):
+        l, k = unit_of(u)
+        mine = r.wg.at[l, k, y]
+        src, dst, peer = (
+            (r.wg.at[l, k, 1 - y], r.yland.at[u], y_peer),
+            (mine, r.zland.at[u], pair_peer),
+            (mine, r.mland.at[u], cross_peer),
+            (mine, r.zland.at[u], pair_peer),
+            (mine, mine, y_peer),
+        )[stage]
+        return remote(src, dst, r.us.at[u, stage], r.ur.at[u, stage], peer)
+
+    def unit_add(u, landed):
+        l, k = unit_of(u)
+        r.wg[l, k, y] = (r.wg[l, k, y].astype(F32) + landed[u].astype(F32)).astype(BF16)
+
+    def unit_stage(u, stage):
+        if stage == 0:
+            unit_copy(u, 0).start()
+        if stage == 1:
+            unit_copy(u, 0).wait_send()
+            pl.semaphore_signal(r.freed, inc=1, device_id=y_peer, device_id_type=MESH)
+            unit_copy(u, 0).wait_recv()
+            unit_add(u, r.yland)
+
+            @pl.when(jnp.logical_not(middle))
+            def _():
+                unit_copy(u, 1).start()
+
+        if stage == 2:
+
+            @pl.when(middle)
+            def _():
+                unit_copy(u, 1).wait_recv()
+                unit_add(u, r.zland)
+                unit_copy(u, 2).start()
+
+        if stage == 3:
+
+            @pl.when(middle)
+            def _():
+                unit_copy(u, 2).wait_recv()
+                unit_copy(u, 2).wait_send()
+                unit_add(u, r.mland)
+                unit_copy(u, 3).start()
+
+        if stage == 4:
+
+            @pl.when(jnp.logical_not(middle))
+            def _():
+                l, k = unit_of(u)
+                unit_copy(u, 1).wait_send()
+                unit_copy(u, 3).wait_recv()
+                r.wg[l, k, y] = r.zland[u]
+
+            pl.semaphore_wait(r.freed, 1)
+            unit_copy(u, 4).start()
+        if stage == 5:
+            l, k = unit_of(u)
+            theirs = r.wg.at[l, k, 1 - y]
+            remote(theirs, theirs, r.us.at[u, 4], r.ur.at[u, 4], y_peer).wait_recv()
+            unit_copy(u, 4).wait_send()
+
+            @pl.when(middle)
+            def _():
+                unit_copy(u, 3).wait_send()
+
+    def tick(m):
+        if not z.reduce:
+            return
+        for stage in reversed(range(6)):
+            u = m - stage
+
+            @pl.when((u >= 0) & (u < z.units * L))
+            def _():
+                unit_stage(u, stage)
 
     def ag_copy(e, full, c, kind):
         chip = other if kind == 2 else xi
@@ -154,7 +262,6 @@
         ag_copy(e, full, c, 2).start()
 
     def rs_copy(e, c, kind):
-        side = 0 if z.single_side else None
         return remote(
             r.stage.at[kind, c],
             r.land.at[r_side(e), kind, c],
@@ -234,13 +341,18 @@
     def flat(v):
         return v.reshape(-1, v.shape[-1])
 
-    w_copies = [
-        pltpu.make_async_copy(
-            r.ffw.at[l, k], r.wffn.at[l, :, pl.ds(k * F, F)], r.wsem.at[l, k]
-        )
-        for l in range(L)
-        for k in range(2)
-    ]
+    r.wmix[...] = jnp.zeros_like(r.wmix)
+    r.wout[...] = jnp.zeros_like(r.wout)
+    w_copies = []
+    for l in range(L):
+        parts = (r.inw.at[l, 0], r.inw.at[l, 1], r.fw.at[l], r.gw.at[l, 0], r.gw.at[l, 1])
+        pairs = [(part, r.wmix.at[l, pl.ds(k * C, ch), :]) for k, part in enumerate(parts)]
+        pairs += [(r.ow.at[l, k], r.wout.at[l, pl.ds(k * C, ch), :]) for k in range(2)]
+        pairs += [(r.ffw.at[l, k], r.wffn.at[l, :, pl.ds(k * F, F)]) for k in range(2)]
+        pairs += [(r.dw.at[l], r.wdown.at[l])]
+        w_copies += [
+            pltpu.make_async_copy(src, dst, r.wsem.at[l, k]) for k, (src, dst) in enumerate(pairs)
+        ]
     for copy in w_copies:
         copy.start()
 
@@ -250,21 +362,15 @@
     col = iota((tokens, tokens), 1)
     place = lax.rem(row, SEGS) * width + row // SEGS
     perm = jnp.where(col == place, 1.0, 0.0).astype(BF16)
-    r.st[0, 0] = mm(perm, r.x[...]).reshape(N, R, D)
+    r.st[0] = mm(perm, r.x[...]).reshape(N, R, D)
     r.grad[...] = mm(perm, r.ct[...]).reshape(N, R, D)
 
     r.ngf[...] = r.ng[...].astype(F32)
-    r.wmix[...] = jnp.zeros_like(r.wmix)
-    r.wout[...] = jnp.zeros_like(r.wout)
     r.par[...] = jnp.zeros_like(r.par)
     r.gacc[...] = jnp.zeros_like(r.gacc)
+    r.wg[:, z.units - 1, 1] = jnp.zeros((L, z.blk, D), BF16)
     r.sacc[...] = jnp.zeros_like(r.sacc)
     for l in range(L):
-        parts = (r.inw.at[l, 0], r.inw.at[l, 1], r.fw.at[l], r.gw.at[l, 0], r.gw.at[l, 1])
-        for k, part in enumerate(parts):
-            r.wmix[l, :, k * C : k * C + ch] = part[...]
-        for k in range(2):
-            r.wout[l, k * C : k * C + ch, :] = r.ow[l, k]
         angle = r.ph[l : l + 1, :]
         turn_cos, turn_sin = jnp.cos(angle), jnp.sin(angle)
         r.par[l, 0:1, 0:ch] = turn_cos
@@ -363,20 +469,25 @@
         def send_mix(c):
             @pl.when(l > 0)
             def _():
-                r.st[l, 0, c] = r.st[l - 1, 1, c] + rs_final(e - 1, r.ffnfull.at[l - 1], c)
-
-            s = r.st[l, 0, c]
+                r.st[2 * l, c] = r.st[2 * l - 1, c] + rs_final(e - 1, r.ffnfull.at[l - 1], c)
+
+            s = r.st[2 * l, c]
             full[xi, c, core] = (s * norm_rows(s) * r.ngf[l, 0:1, :]).astype(BF16)
             ag_start(e, full, c)
 
         loop(N, send_mix)
 
+        @pl.when(l == 0)
+        def _():
+            for copy in w_copies:
+                copy.wait()
+
         r.seg[0:2] = jnp.zeros((2, 2, 2, SEGS, C), F32)
         r.seg[2] = jnp.ones((2, 2, SEGS, C), F32)
 
         def project(j):
             chip, c = chip_chunk(j, ascending, True)
-            proj = mm(flat(full[chip, c]), r.wmix[l])
+            proj = mm_nt(flat(full[chip, c]), r.wmix[l])
             r.proj[l, chip, c] = proj.reshape(2, R, 5 * C)
             in_re, in_im, pre = proj[:, 0:C], proj[:, C : 2 * C], proj[:, 2 * C : 3 * C]
             rate = lower + (1.0 - lower) * sigmoid(pre)
@@ -430,17 +541,12 @@
         full2 = r.ffnfull.at[l]
 
         def send_ffn(c):
-            s = r.st[l, 0, c] + rs_final(e, full, c)
-            r.st[l, 1, c] = s
+            s = r.st[2 * l, c] + rs_final(e, full, c)
+            r.st[2 * l + 1, c] = s
             full2[xi, c, core] = (s * norm_rows(s) * r.ngf[l, 1:2, :]).astype(BF16)
             ag_start(e2, full2, c)
 
         loop(N, send_ffn)
-
-        @pl.when(l == 0)
-        def _():
-            for copy in w_copies:
-                copy.wait()
 
         def feed(j):
             chip, c = chip_chunk(j, ascending, True)
@@ -449,7 +555,7 @@
             gate, up = both[:, 0:F], both[:, F : 2 * F]
             hidden = (gate * sigmoid(gate) * up).astype(BF16)
             r.hidden[l, chip, c] = hidden.reshape(2, R, F)
-            r.psc[...] = mm(hidden, r.dw[l]).reshape(2, R, D)
+            r.psc[...] = mm(hidden, r.wdown[l]).reshape(2, R, D)
 
             @pl.when(j < N)
             def _():
@@ -470,14 +576,14 @@
 
     def last_sum(c):
         e = 2 * L - 1
-        r.st[L, 0, c] = r.st[L - 1, 1, c] + rs_final(e, r.ffnfull.at[L - 1], c)
+        r.st[2 * L, c] = r.st[2 * L - 1, c] + rs_final(e, r.ffnfull.at[L - 1], c)
 
     loop(N, last_sum)
     unperm = perm
-    r.out[...] = mm_tn(unperm, r.st[L, 0].reshape(tokens, D).astype(BF16)).astype(BF16)
+    r.out[...] = mm_tn(unperm, r.st[2 * L].reshape(tokens, D).astype(BF16)).astype(BF16)
 
     def norm_back(l, which, c, grad_out):
-        s = r.st[l, which, c]
+        s = r.st[2 * l + which, c]
         scale = norm_rows(s)
         r.gacc[l, which] += fold(grad_out * s * scale)
         scaled = grad_out * r.ngf[l, which : which + 1, :]
@@ -489,23 +595,27 @@
     def backward_layer(step):
         l = L - 1 - step
         e = 2 * L + 2 * step
-        full = r.gfull.at[l, 0]
+        full = r.gfull.at[0]
 
         def send_ffn(j):
             c = descending(j)
 
             @pl.when(step > 0)
             def _():
-                norm_back(l + 1, 0, c, rs_final(e - 1, r.gfull.at[l + 1, 1], c))
+                norm_back(l + 1, 0, c, rs_final(e - 1, r.gfull.at[1], c))
 
             full[xi, c, core] = r.grad[c].astype(BF16)
             ag_start(e, full, c)
 
         loop(N, send_ffn)
 
+        @pl.when(step > 0)
+        def _():
+            tick((step - 1) * z.units + 7)
+
         def feed_back(j):
             chip, c = chip_chunk(j, descending, True)
-            g_hidden = mm_nt(flat(full[chip, c]), r.dw[l])
+            g_hidden = mm_nt(flat(full[chip, c]), r.wdown[l])
             both = flat(r.gup[l, chip, c]).astype(F32)
             gate, up = both[:, 0:F], both[:, F : 2 * F]
             s = sigmoid(gate)
@@ -527,25 +637,35 @@
             def _():
                 rs_pass(e, descending(j - N - 1))
 
+            @pl.when((step > 0) & (lax.rem(j, N) == N // 2))
+            def _():
+                tick((step - 1) * z.units + 8 + j // N)
+
         gather_loop(e, full, descending, feed_back)
         rs_pass(e, 0)
 
-        def down_tile(i):
-            cols = pl.ds(pl.multiple_of(i * LANES, LANES), LANES)
-            r.gdown[l, cols, :] = mm_tn(flat(r.hidden[l, :, :, :, :, cols]), flat(full[...])).astype(BF16)
-
-        loop(F // LANES, down_tile)
-
         def ffn_tile(i):
-            cols = pl.ds(pl.multiple_of(i * LANES, LANES), LANES)
-            r.gffn[l, cols, :] = mm_tn(flat(r.ffnfull[l, :, :, :, :, cols]), flat(r.dgu[...])).astype(BF16)
-
-        loop(D // LANES, ffn_tile)
+            cols = pl.ds(pl.multiple_of(i * F, LANES), F)
+
+            @pl.when(i == 0)
+            def _():
+                part = mm_tn(flat(r.hidden[l]), flat(full[...])).astype(BF16)
+                r.wg[l, 0 : z.fu] = part.reshape(z.fu, 2, z.blk, D)
+
+            @pl.when(i > 0)
+            def _():
+                cols = pl.ds(pl.multiple_of((i - 1) * F, LANES), F)
+                part = mm_tn(flat(r.ffnfull[l, :, :, :, :, cols]), flat(r.dgu[...])).astype(BF16)
+                r.wg[l, pl.ds(i * z.fu, z.fu)] = part.reshape(z.fu, 2, z.blk, D)
+
+        loop(1 + D // F, ffn_tile)
+        first_tick = step * z.units
+        tick(first_tick)
 
         turn_cos, turn_sin, lower = r.par[l, 0:1, :], r.par[l, 1:2, :], r.par[l, 2:3, :]
         gain_re, gain_im = r.par[l, 3:4, :], r.par[l, 4:5, :]
         e2 = e + 1
-        full2 = r.gfull.at[l, 1]
+        full2 = r.gfull.at[1]
 
         def send_mix(j):
             c = descending(j)
@@ -554,6 +674,7 @@
             ag_start(e2, full2, c)
 
         loop(N, send_mix)
+        tick(first_tick + 1)
         r.seg[0:2] = jnp.zeros((2, 2, 2, SEGS, C), F32)
 
         def mix_back(j):
@@ -578,6 +699,10 @@
             pre = flat(r.proj[l, chip, c, :, :, 2 * C : 3 * C])
             r.keep[chip, c] = (lower + (1.0 - lower) * sigmoid(pre)).reshape(2, R, C)
             scan_back_local(l, chip, c, turn_cos, turn_sin)
+
+            @pl.when(lax.rem(j, N) == N // 2)
+            def _():
+                tick(first_tick + 2 + j // N)
 
         gather_loop(e2, full2, descending, mix_back)
         carry_over(l, True)
@@ -605,7 +730,7 @@
             r.dproj[chip, c, :, :, 0:C] = d_re.astype(BF16).reshape(2, R, C)
             r.dproj[chip, c, :, :, C : 2 * C] = d_im.astype(BF16).reshape(2, R, C)
             r.dproj[chip, c, :, :, 2 * C : 3 * C] = d_f.astype(BF16).reshape(2, R, C)
-            r.psc[...] = mm_nt(flat(r.dproj[chip, c]), r.wmix[l]).reshape(2, R, D)
+            r.psc[...] = mm(flat(r.dproj[chip, c]), r.wmix[l]).reshape(2, R, D)
 
             @pl.when(j < N)
             def _():
@@ -619,37 +744,72 @@
             def _():
                 rs_own(e2, c)
 
+            @pl.when(lax.rem(j, N) == N // 2)
+            def _():
+                tick(first_tick + 4 + j // N)
+
         loop(2 * N, scan_back)
 
+        base_unit = z.units - 4
+
         def out_tile(i):
-            cols = pl.ds(pl.multiple_of(i * LANES, LANES), LANES)
-            r.gout[l, cols, :] = mm_tn(flat(r.mixed[l, :, :, :, :, cols]), flat(full2[...])).astype(BF16)
-
-        loop(2 * C // LANES, out_tile)
+            cols = pl.ds(pl.multiple_of(i * C, LANES), C)
+            part = mm_tn(flat(r.mixed[l, :, :, :, :, cols]), flat(full2[...])).astype(BF16)
+            r.wg[l, base_unit, i] = part[0:ch]
+
+        loop(2, out_tile)
 
         def mix_tile(i):
-            cols = pl.ds(pl.multiple_of(i * LANES, LANES), LANES)
-            r.gmix[l, cols, :] = mm_tn(flat(r.mixfull[l, :, :, :, :, cols]), flat(r.dproj[...])).astype(BF16)
-
-        loop(D // LANES, mix_tile)
+            k = lax.rem(i + 3, 5)
+            cols = pl.ds(pl.multiple_of(k * C, LANES), C)
+            part = mm_tn(flat(r.dproj[:, :, :, :, cols]), flat(r.mixfull[l])).astype(BF16)
+            r.wg[l, base_unit + 1 + i // 2, lax.rem(i, 2)] = part[0:ch]
+
+        loop(5, mix_tile)
+        tick(first_tick + 6)
 
     loop(L, backward_layer)
 
     def last_grad(j):
         c = descending(j)
-        norm_back(0, 0, c, rs_final(4 * L - 1, r.gfull.at[0, 1], c))
+        norm_back(0, 0, c, rs_final(4 * L - 1, r.gfull.at[1], c))
 
     loop(N, last_grad)
     r.ig[...] = mm_tn(perm, r.grad[...].reshape(tokens, D).astype(BF16)).astype(BF16)
+
+    r.swork[...] = jnp.zeros_like(r.swork)
     for l in range(L):
         for which in range(2):
-            r.gains[2 * l + which : 2 * l + which + 1, :] = jnp.sum(r.gacc[l, which], axis=0, keepdims=True)
+            at = 2 * l + which
+            r.swork[at : at + 1, :] = jnp.sum(r.gacc[l, which], axis=0, keepdims=True)
+
+    def swap_sum(k, peer, first):
+        copy = remote(r.swork, r.sland.at[k], r.ss.at[k], r.sr.at[k], peer)
+        copy.start()
+        copy.wait()
+        r.swork[...] = r.swork[...] + r.sland[k]
+
+    swap_sum(0, sib, True)
+    swap_sum(1, xnb, True)
+    for l in range(L):
         for k in range(4):
             value = jnp.sum(r.sacc[l, k], axis=0, keepdims=True)
             if k == 3:
                 lower = r.par[l, 2:3, :]
                 value = value * lower * (1.0 - lower)
-            r.small[4 * l + k : 4 * l + k + 1, :] = value
+            at = 2 * L + 4 * l + k
+            r.swork[at : at + 1, 0:C] = value
+    if z.reduce:
+        swap_sum(2, y_peer, False)
+        swap_sum(3, pair_peer, False)
+        swap_sum(4, cross_peer, False)
+        start = (L - 1) * z.units + 7
+
+        def drain(i):
+            tick(start + i)
+
+        loop(z.units + 5 - 7, drain)
+    r.sums[...] = r.swork[...]
 
 
 def local(*args):
@@ -658,52 +818,61 @@
     ch = fw.shape[2]
     F = dw.shape[1]
     C = -(-ch // LANES) * LANES
-    z = types.SimpleNamespace(L=L, D=D, C=C, F=F, ch=ch, R=x.shape[0] // CHUNKS, single_side=False)
+    n_dp = lax.axis_size("dp")
+    reduce = n_dp % 8 == 0
+    fu = F // (2 * ch)
+    units = fu * (1 + D // F) + 4
+    z = types.SimpleNamespace(
+        L=L, D=D, C=C, F=F, ch=ch, R=x.shape[0] // CHUNKS, reduce=reduce, blk=ch, fu=fu, units=units
+    )
     names, scratch = scratch_of(z)
     vmem = pl.BlockSpec(memory_space=pltpu.VMEM)
     in_specs = [vmem] * 12
-    in_specs[10] = pl.BlockSpec(memory_space=pl.ANY)
+    for k in (3, 4, 5, 6, 10, 11):
+        in_specs[k] = pl.BlockSpec(memory_space=pl.ANY)
     shape = jax.ShapeDtypeStruct
-    out, ig, gffn, gdown, gmix, gout, small, gains = pl.pallas_call(
+    out, ig, wg, sums = pl.pallas_call(
         functools.partial(mega, z, names),
         out_shape=(
             shape(x.shape, BF16),
             shape(x.shape, BF16),
-            shape((L, D, 2 * F), BF16),
-            shape((L, F, D), BF16),
-            shape((L, D, 5 * C), BF16),
-            shape((L, 2 * C, D), BF16),
-            shape((4 * L, C), F32),
-            shape((2 * L, D), F32),
+            shape((L, units, 2, ch, D), BF16),
+            shape((2 * SEGS, D), F32),
         ),
         in_specs=in_specs,
-        out_specs=[vmem] * 8,
+        out_specs=[vmem] * 4,
         scratch_shapes=scratch,
         compiler_params=pltpu.CompilerParams(
             collective_id=0, has_side_effects=True, vmem_limit_bytes=VMEM_BYTES
         ),
         name="layers",
-    )(x, ct, ng, inw, fw, gw, ow, ph, bl, gg, ffw, dw)
-
-    gffn, gdown, gmix, gout, small = lax.psum((gffn, gdown, gmix, gout, small), "dp")
-    gains = lax.psum(gains, ("dp", "tensor")).reshape(L, 2, D)
+    )(x, ct, ng, jnp.swapaxes(inw, 2, 3), jnp.swapaxes(fw, 1, 2), jnp.swapaxes(gw, 2, 3), ow, ph, bl, gg, ffw, dw)
+
+    if not reduce:
+        wg, sums = lax.psum((wg, sums), "dp")
+    elif n_dp > 8:
+        groups = [list(range(k, n_dp, 8)) for k in range(8)]
+        wg, sums = lax.psum((wg, sums), "dp", axis_index_groups=groups)
+    wg = wg.astype(F32)
+    gains = sums[: 2 * L].reshape(L, 2, D)
     piece = D // lax.axis_size("tensor")
     gains = lax.dynamic_slice_in_dim(gains, lax.axis_index("tensor") * piece, piece, 2)
-    gmix = gmix.astype(F32).reshape(L, D, 5, C)[..., :ch]
-    small = small.reshape(L, 4, C)[..., :ch]
+    small = sums[2 * L : 6 * L, :ch].reshape(L, 4, ch)
+    g_down = wg[:, :fu].reshape(L, F, D)
+    g_ffn = wg[:, fu : units - 4].reshape(L, D, 2 * F)
     return (
         out,
         ig,
         gains,
-        jnp.stack([gmix[:, :, 0], gmix[:, :, 1]], axis=1),
-        gmix[:, :, 2],
-        jnp.stack([gmix[:, :, 3], gmix[:, :, 4]], axis=1),
-        gout.astype(F32).reshape(L, 2, C, D)[:, :, :ch],
+        jnp.swapaxes(wg[:, units - 2], 2, 3),
+        jnp.swapaxes(wg[:, units - 1, 0], 1, 2),
+        jnp.swapaxes(wg[:, units - 3], 2, 3),
+        wg[:, units - 4],
         small[:, 2],
         small[:, 3],
         small[:, 0:2],
-        jnp.stack([gffn[:, :, :F], gffn[:, :, F:]], axis=1).astype(F32),
-        gdown.astype(F32),
+        jnp.stack([g_ffn[:, :, :F], g_ffn[:, :, F:]], axis=1),
+        g_down,
     )
 
 

time: 427 us -> 279 us (0.65)
  waiting for transfers between devices: 152 us -> 0 us
  Pallas kernels: 174 us -> 262 us
  blocking collectives: 62.1 us -> 0 us
  between operations: 14.1 us -> 0.69 us
  local copies, waits for them, and re-layouts: 19.3 us -> 9.94 us
    psum x1 -> x0, waiting for transfers between devices: 152 us -> none  [local(): lax.psum((gffn, gdown, gmix, gout, small), 'dp')]
    pallas_call x1, Pallas kernels: 174 us -> 262 us  [local(): pl.pallas_call(functools.partial(mega, z, names), out_shape=(shape(x.shap...]
    psum x2 -> x0, blocking collectives: 62.1 us -> none  [the longest x1 39.8 us: local(): gains = lax.psum(gains, ('dp', 'tensor')).reshape(L, 2, D)]
    unnamed x26 -> x10, local copies, waits for them, and re-layouts: 12.2 us -> 1.51 us
  transfers between devices with their start and end apart: 1 -> 0, of which waited for: 1 -> 0; matrix products, arithmetic and copies ran while one was open for 0% -> 0% of each run, Pallas kernels for 0% -> 0%
where the time goes in v2:
time: 279 us
  Pallas kernels  262 us (94%)
  local copies, waits for them, and re-layouts  9.94 us (4%)
  other arithmetic  6.83 us (2%)
    pallas_call x1, Pallas kernels, local(): pl.pallas_call(functools.partial(mega, z, names), out_shape=(shape(x.shap...  262 us

profile of v2, /device:TPU:0, one launch (start us, length us, event | category | flops | bytes accessed | tf_op | source)
XLA Modules:
  0.0 279.0 jit_solution(14979112759731107651)
XLA Ops:
  0.6 261.5 %layers.1 = (bf16[256,768]{1,0:T(8,128)(2,1)}, bf16[256,768]{1,0:T(8,128)(2,1)}, bf16[2,10,2,96,768]{4,3,2,1,0:T(8,128)(2,1)}, f32[16,768]{1,0:T(8,128)}) custom-call(bf16[256,768]{1,0:T(8,128)(2,1)} %refs_0_.1, bf16[256,768]{1,0:T(8,128)(2,1)} %refs_1_.1, bf16[2,2,768]{2,1,0:T(2,128)(2,1)} %refs_2_.1, bf16[2,2,96,768]{3,2,1,0:T(8,128)(2,1)} %bitcast.32, ...), custom_call_target="tpu_custom_call" | custom-call | tf_op jit(solution)/shard_map/layers/pallas_call | solution.py:834
  262.2 0.7 slice.39
  263.0 0.7 constant_dynamic-slice_fusion
  263.6 0.0 slice-start
  263.6 0.0 slice-start.1
  263.6 4.3 %convert_element_type.3 = f32[2,10,2,96,768]{4,3,2,1,0:T(8,128)S(1)} convert(bf16[2,10,2,96,768]{4,3,2,1,0:T(8,128)(2,1)} %get-tuple-element.19) | non-fusion elementwise | flops 2949120 | bytes 17694720 | tf_op jit(solution)/shard_map/convert_element_type | solution.py:856
  268.0 1.9 slice_bitcast_fusion.2
  269.9 0.9 slice_bitcast_fusion.5
  270.7 0.7 slice.44
  271.4 0.6 fusion
  272.0 0.6 slice.58
  272.6 0.0 slice-done
  272.6 0.0 slice-done.1
  272.6 0.5 slice.59
  273.1 0.3 slice_bitcast_fusion.1
  273.4 2.5 pad_maximum_fusion
  275.9 0.0 copy-start.1
  275.9 0.0 copy-start
  275.9 1.6 slice.62
  277.5 0.0 copy-done.1
  277.5 0.7 copy.27
  278.3 0.0 copy-done
  278.3 0.7 copy.28
  (2 shorter events, 0.0 us)
Async XLA Ops:
  263.6 8.9 %slice-start = ((s8[5898240]{0:T(1024)(128)(4,1)}), s8[4194304]{0:T(1024)(128)(4,1)S(1)}, s32[]{:S(2)}) async-start(s8[5898240]{0:T(1024)(128)(4,1)} %bitcast.28), calls=%async_computation | async-start | bytes 8388608
  263.6 8.9 %slice-start.1 = ((s8[5898240]{0:T(1024)(128)(4,1)}), s8[1703936]{0:T(1024)(128)(4,1)S(1)}, s32[]{:S(2)}) async-start(s8[5898240]{0:T(1024)(128)(4,1)} %bitcast.28), calls=%async_computation.1 | async-start | bytes 3407872
  275.9 1.6 copy-start.1
  275.9 2.4 copy-start

commit v3 on v2

--- a/solution.py
+++ b/solution.py
@@ -18,6 +18,10 @@
 LANES = 128
 SEGS = 8
 CHUNKS = 4
+LAG = 2
+UNIT_PIECES = 3
+PIECES = 2
+SLOTS = 10
 VMEM_BYTES = 63 * 1024 * 1024
 
 
@@ -47,6 +51,13 @@
 
 def iota(shape, dim):
     return lax.broadcasted_iota(jnp.int32, shape, dim)
+
+
+def permutation(tokens):
+    width = tokens // SEGS
+    row = iota((tokens, tokens), 0)
+    place = lax.rem(row, SEGS) * width + row // SEGS
+    return jnp.where(iota((tokens, tokens), 1) == place, 1.0, 0.0).astype(BF16)
 
 
 def scratch_of(z):
@@ -60,7 +71,7 @@
         par=((L, 8, C), F32),
         ngf=((L, 2, D), F32),
         gsum=((C, C), BF16),
-        st=((2 * L + 1, *own, D), F32),
+        st=((2 * L, *own, D), F32),
         mixfull=((L, *rows, D), BF16),
         ffnfull=((L, *rows, D), BF16),
         gfull=((2, *rows, D), BF16),
@@ -81,19 +92,21 @@
         dproj=((*rows, 5 * C), BF16),
         psc=((2, R, D), F32),
         xpart=((*own, D), F32),
-        opart=((*own, D), F32),
+        opart=((2, *own, D), F32),
         grad=((*own, D), F32),
-        stage=((3, *own, D), BF16),
+        stage=((2, 3, *own, D), BF16),
         land=((2, 3, *own, D), BF16),
         gacc=((L, 2, SEGS, D), F32),
         sacc=((L, 4, SEGS, C), F32),
         wdown=((L, F, D), BF16),
+        wg=((L, z.units, 2, z.blk, D), BF16),
         swork=((2 * SEGS, D), F32),
         sland=((5, 2 * SEGS, D), F32),
     )
     if z.reduce:
-        unit = (z.units * L, z.blk, D)
-        bufs.update(yland=(unit, BF16), zland=(unit, BF16), mland=(unit, BF16))
+        unit = (SLOTS, z.blk, D)
+        bufs.update(yland=(unit, BF16), mland=(unit, BF16))
+        bufs.update(zland=((SLOTS // 2, z.blk, D), BF16), zfold=((SLOTS // 2, 2, z.blk, D), BF16))
     sems = dict(
         ags=(4 * L, 3, N),
         agr=(4 * L, 3, N),
@@ -102,6 +115,7 @@
         wsem=(L, 10),
         ss=(5,),
         sr=(5,),
+        outs=(z.units * L,),
     )
     if z.reduce:
         sems.update(us=(z.units * L, 5), ur=(z.units * L, 5))
@@ -109,12 +123,12 @@
     shapes = [pltpu.VMEM(s, d) for s, d in bufs.values()]
     shapes += [pltpu.SemaphoreType.DMA(s) for s in sems.values()]
     names.append("freed")
-    shapes.append(pltpu.SemaphoreType.REGULAR)
+    shapes.append(pltpu.SemaphoreType.REGULAR((3,)))
     return names, shapes
 
 
 IN_NAMES = ("x", "ct", "ng", "inw", "fw", "gw", "ow", "ph", "bl", "gg", "ffw", "dw")
-OUT_NAMES = ("out", "ig", "wg", "sums")
+OUT_NAMES = ("out", "ig", "wgout", "sums")
 
 
 def mega(z, names, *refs):
@@ -151,101 +165,205 @@
         pl.semaphore_signal(barrier, inc=1, device_id=peer, device_id_type=MESH)
     pl.semaphore_wait(barrier, len(peers))
 
-    def remote(src, dst, send, recv, peer):
-        return pltpu.make_async_remote_copy(
-            src_ref=src,
-            dst_ref=dst,
-            send_sem=send,
-            recv_sem=recv,
-            device_id=peer if isinstance(peer, tuple) else (dp, peer),
-            device_id_type=MESH,
+    def remote(src, dst, send, recv, peer, pieces=1):
+        def copy(source, target):
+            return pltpu.make_async_remote_copy(
+                src_ref=source,
+                dst_ref=target,
+                send_sem=send,
+                recv_sem=recv,
+                device_id=peer if isinstance(peer, tuple) else (dp, peer),
+                device_id_type=MESH,
+            )
+
+        def start():
+            lead = src.shape[0] if len(src.shape) == 3 else 1
+            size = src.shape[-2] // pieces
+            for first in range(lead):
+                for k in range(pieces):
+                    at = pl.ds(k * size, size)
+                    if len(src.shape) == 3:
+                        copy(src.at[first, at], dst.at[first, at]).start()
+                    else:
+                        copy(src.at[at], dst.at[at]).start()
+
+        whole = copy(src, dst)
+        return types.SimpleNamespace(
+            start=start, wait_recv=whole.wait_recv, wait_send=whole.wait_send, wait=whole.wait
         )
 
     def unit_of(u):
         return L - 1 - u // z.units, lax.rem(u, z.units)
 
-    def unit_copy(u, stage):
+    half = line // 2
+
+    def unit_copy(u, stage, even):
         l, k = unit_of(u)
+        slot = lax.rem(u, SLOTS)
         mine = r.wg.at[l, k, y]
-        src, dst, peer = (
-            (r.wg.at[l, k, 1 - y], r.yland.at[u], y_peer),
-            (mine, r.zland.at[u], pair_peer),
-            (mine, r.mland.at[u], cross_peer),
-            (mine, r.zland.at[u], pair_peer),
-            (mine, mine, y_peer),
-        )[stage]
-        return remote(src, dst, r.us.at[u, stage], r.ur.at[u, stage], peer)
-
-    def unit_add(u, landed):
+        if even:
+            part = r.wg.at[l, k, half]
+            src, dst, peer = (
+                (r.wg.at[l, k], r.zfold.at[slot // 2], pair_peer),
+                (r.wg.at[l, k, 1 - half], r.mland.at[slot], cross_peer),
+                (part, r.yland.at[slot], y_peer),
+                (part, part, cross_peer),
+                (r.wg.at[l, k], r.wg.at[l, k], pair_peer),
+            )[stage]
+        else:
+            src, dst, peer = (
+                (r.wg.at[l, k, 1 - y], r.yland.at[slot], y_peer),
+                (mine, r.zland.at[slot // 2], pair_peer),
+                (mine, r.mland.at[slot], cross_peer),
+                (mine, r.zland.at[slot // 2], pair_peer),
+                (mine, mine, y_peer),
+            )[stage]
+        return remote(src, dst, r.us.at[u, stage], r.ur.at[u, stage], peer, UNIT_PIECES)
+
+    def unit_land(u, stage, ref, peer):
+        return remote(ref, ref, r.us.at[u, stage], r.ur.at[u, stage], peer)
+
+    def unit_add(u, part, landed):
         l, k = unit_of(u)
-        r.wg[l, k, y] = (r.wg[l, k, y].astype(F32) + landed[u].astype(F32)).astype(BF16)
-
-    def unit_stage(u, stage):
+        r.wg[l, k, part] = (r.wg[l, k, part].astype(F32) + landed.astype(F32)).astype(BF16)
+
+    def tell(sem, peer):
+        pl.semaphore_signal(sem, inc=1, device_id=peer, device_id_type=MESH)
+
+    def on_middle(body):
+        pl.when(middle)(body)
+
+    def on_end(body):
+        pl.when(jnp.logical_not(middle))(body)
+
+    def odd_stage(u, stage):
+        copy = lambda n: unit_copy(u, n, False)
+        slot = lax.rem(u, SLOTS)
+        l, k = unit_of(u)
         if stage == 0:
-            unit_copy(u, 0).start()
+            copy(0).start()
         if stage == 1:
-            unit_copy(u, 0).wait_send()
-            pl.semaphore_signal(r.freed, inc=1, device_id=y_peer, device_id_type=MESH)
-            unit_copy(u, 0).wait_recv()
-            unit_add(u, r.yland)
-
-            @pl.when(jnp.logical_not(middle))
-            def _():
-                unit_copy(u, 1).start()
-
+            copy(0).wait_send()
+            tell(r.freed.at[0], y_peer)
+            copy(0).wait_recv()
+            unit_add(u, y, r.yland[slot])
+            on_end(lambda: copy(1).start())
         if stage == 2:
 
-            @pl.when(middle)
-            def _():
-                unit_copy(u, 1).wait_recv()
-                unit_add(u, r.zland)
-                unit_copy(u, 2).start()
+            @on_middle
+            def _():
+                copy(1).wait_recv()
+                unit_add(u, y, r.zland[slot // 2])
+                copy(2).start()
 
         if stage == 3:
 
-            @pl.when(middle)
-            def _():
-                unit_copy(u, 2).wait_recv()
-                unit_copy(u, 2).wait_send()
-                unit_add(u, r.mland)
-                unit_copy(u, 3).start()
+            @on_middle
+            def _():
+                copy(2).wait_recv()
+                copy(2).wait_send()
+                unit_add(u, y, r.mland[slot])
+                copy(3).start()
 
         if stage == 4:
 
-            @pl.when(jnp.logical_not(middle))
-            def _():
-                l, k = unit_of(u)
-                unit_copy(u, 1).wait_send()
-                unit_copy(u, 3).wait_recv()
-                r.wg[l, k, y] = r.zland[u]
-
-            pl.semaphore_wait(r.freed, 1)
-            unit_copy(u, 4).start()
+            @on_end
+            def _():
+                copy(1).wait_send()
+                copy(3).wait_recv()
+                r.wg[l, k, y] = r.zland[slot // 2]
+
+            pl.semaphore_wait(r.freed.at[0], 1)
+            copy(4).start()
         if stage == 5:
-            l, k = unit_of(u)
-            theirs = r.wg.at[l, k, 1 - y]
-            remote(theirs, theirs, r.us.at[u, 4], r.ur.at[u, 4], y_peer).wait_recv()
-            unit_copy(u, 4).wait_send()
-
-            @pl.when(middle)
-            def _():
-                unit_copy(u, 3).wait_send()
+            unit_land(u, 4, r.wg.at[l, k, 1 - y], y_peer).wait_recv()
+            copy(4).wait_send()
+            on_middle(lambda: copy(3).wait_send())
+            unit_out(u).start()
+
+    def even_stage(u, stage):
+        copy = lambda n: unit_copy(u, n, True)
+        slot = lax.rem(u, SLOTS)
+        l, k = unit_of(u)
+        if stage == 0:
+            on_end(lambda: copy(0).start())
+        if stage == 1:
+
+            @on_end
+            def _():
+                copy(0).wait_send()
+                tell(r.freed.at[1], pair_peer)
+
+            @on_middle
+            def _():
+                copy(0).wait_recv()
+                for part in range(2):
+                    unit_add(u, part, r.zfold[slot // 2, part])
+                copy(1).start()
+
+        if stage == 2:
+
+            @on_middle
+            def _():
+                copy(1).wait_send()
+                tell(r.freed.at[2], cross_peer)
+                copy(1).wait_recv()
+                unit_add(u, half, r.mland[slot])
+                copy(2).start()
+
+        if stage == 3:
+
+            @on_middle
+            def _():
+                copy(2).wait_send()
+                copy(2).wait_recv()
+                unit_add(u, half, r.yland[slot])
+                pl.semaphore_wait(r.freed.at[2], 1)
+                copy(3).start()
+
+        if stage == 4:
+
+            @on_middle
+            def _():
+                unit_land(u, 3, r.wg.at[l, k, 1 - half], cross_peer).wait_recv()
+                pl.semaphore_wait(r.freed.at[1], 1)
+                copy(4).start()
+
+        if stage == 5:
+            on_end(lambda: copy(4).wait_recv())
+
+            @on_middle
+            def _():
+                copy(3).wait_send()
+                copy(4).wait_send()
+
+            unit_out(u).start()
+
+    def unit_out(u):
+        l, k = unit_of(u)
+        return pltpu.make_async_copy(r.wg.at[l, k], r.wgout.at[l, k], r.outs.at[u])
 
     def tick(m):
         if not z.reduce:
             return
         for stage in reversed(range(6)):
-            u = m - stage
-
-            @pl.when((u >= 0) & (u < z.units * L))
-            def _():
-                unit_stage(u, stage)
+            u = m - LAG * stage
+
+            there = (u >= 0) & (u < z.units * L)
+
+            @pl.when(there & (lax.rem(u, 2) == 1))
+            def _():
+                odd_stage(u, stage)
+
+            @pl.when(there & (lax.rem(u, 2) == 0))
+            def _():
+                even_stage(u, stage)
 
     def ag_copy(e, full, c, kind):
         chip = other if kind == 2 else xi
         peer = xnb if kind == 0 else sib
         ref = full.at[chip, c, core]
-        return remote(ref, ref, r.ags.at[e, kind, c], r.agr.at[e, kind, c], peer)
+        return remote(ref, ref, r.ags.at[e, kind, c], r.agr.at[e, kind, c], peer, PIECES if kind == 0 else 1)
 
     def ag_landing(e, full, c, kind):
         chip = xi if kind == 1 else other
@@ -263,65 +381,100 @@
 
     def rs_copy(e, c, kind):
         return remote(
-            r.stage.at[kind, c],
+            r.stage.at[r_side(e), kind, c],
             r.land.at[r_side(e), kind, c],
             r.rss.at[e, kind, c],
             r.rsr.at[e, kind, c],
             xnb if kind == 1 else sib,
+            PIECES if kind == 1 else 1,
         )
 
     def r_side(e):
         return e // (2 * L)
 
     def rs_other(e, c):
-        r.stage[0, c] = r.psc[1 - core].astype(BF16)
+        r.stage[r_side(e), 0, c] = r.psc[1 - core].astype(BF16)
         rs_copy(e, c, 0).start()
         r.xpart[c] = r.psc[core]
 
     def rs_pass(e, c):
         rs_copy(e, c, 0).wait_recv()
-        r.stage[1, c] = (r.xpart[c] + r.land[r_side(e), 0, c].astype(F32)).astype(BF16)
+        r.stage[r_side(e), 1, c] = (r.xpart[c] + r.land[r_side(e), 0, c].astype(F32)).astype(BF16)
         rs_copy(e, c, 1).start()
 
     def rs_own(e, c):
-        r.stage[2, c] = r.psc[1 - core].astype(BF16)
+        r.stage[r_side(e), 2, c] = r.psc[1 - core].astype(BF16)
         rs_copy(e, c, 2).start()
-        r.opart[c] = r.psc[core]
+        r.opart[r_side(e), c] = r.psc[core]
 
     def rs_final(e, full, c):
         rs_copy(e, c, 2).wait_recv()
         rs_copy(e, c, 1).wait_recv()
         side = r_side(e)
-        total = r.opart[c] + r.land[side, 2, c].astype(F32) + r.land[side, 1, c].astype(F32)
+        total = r.opart[side, c] + r.land[side, 2, c].astype(F32) + r.land[side, 1, c].astype(F32)
         for kind in range(3):
             rs_copy(e, c, kind).wait_send()
             ag_copy(e, full, c, kind).wait_send()
         return total
 
-    def gather_loop(e, full, order, stage):
-        def step(j):
-            @pl.when(j < N)
-            def _():
-                ag_landing(e, full, order(j), 1).wait_recv()
-
-            @pl.when((j >= N - 1) & (j < 2 * N - 1))
-            def _():
-                ag_take_x(e, full, order(j - N + 1))
-
-            @pl.when(j >= N)
-            def _():
-                ag_landing(e, full, order(j - N), 2).wait_recv()
-
-            stage(j)
+    def exchange_loop(e, full, order, send, stage, early=None):
+        def when_late(cond, body):
+            pl.when(cond if early is None else cond & jnp.logical_not(early))(body)
+
+        send(order(0))
+        if early is not None:
+
+            @pl.when(early)
+            def _():
+                def take(c):
+                    ag_landing(e, full, c, 1).wait_recv()
+                    ag_landing(e, full, c, 2).wait_recv()
+
+                loop(N, take)
+
+        def step(i):
+            @pl.when(i + 1 < N)
+            def _():
+                send(order(i + 1))
+
+            def take_sib():
+                ag_landing(e, full, order(i), 1).wait_recv()
+
+            def take_x():
+                ag_take_x(e, full, order(i - N + 1))
+
+            def take_far():
+                ag_landing(e, full, order(i - N), 2).wait_recv()
+
+            when_late(i < N, take_sib)
+            when_late((i >= N - 1) & (i < 2 * N - 1), take_x)
+            when_late(i >= N, take_far)
+            stage(i)
 
         loop(2 * N, step)
 
-    def chip_chunk(j, order, own_first):
-        first = j < N
-        chunk = order(jnp.where(first, j, j - N))
-        if own_first:
-            return jnp.where(first, xi, other), chunk
-        return jnp.where(first, other, xi), chunk
+    def chip_chunk(i, order, own_first):
+        first = i < N
+        chunk = order(jnp.where(first, i, i - N))
+        return jnp.where(first == own_first, xi, other), chunk
+
+    def rs_step(e, i, order, own_first):
+        first = i < N
+        chunk = order(jnp.where(first, i, i - N))
+
+        @pl.when(first == own_first)
+        def _():
+            rs_own(e, chunk)
+
+        @pl.when(first != own_first)
+        def _():
+            rs_other(e, chunk)
+
+        behind = jnp.where(own_first, i - N, i) - 1
+
+        @pl.when((behind >= 0) & (behind < N))
+        def _():
+            rs_pass(e, order(behind))
 
     ascending = lambda j: j
     descending = lambda j: N - 1 - j
@@ -341,8 +494,6 @@
     def flat(v):
         return v.reshape(-1, v.shape[-1])
 
-    r.wmix[...] = jnp.zeros_like(r.wmix)
-    r.wout[...] = jnp.zeros_like(r.wout)
     w_copies = []
     for l in range(L):
         parts = (r.inw.at[l, 0], r.inw.at[l, 1], r.fw.at[l], r.gw.at[l, 0], r.gw.at[l, 1])
@@ -357,15 +508,28 @@
         copy.start()
 
     tokens = N * R
+    r.st[0] = mm(permutation(tokens), r.x[...]).reshape(N, R, D)
+    r.ngf[...] = r.ng[...].astype(F32)
+
+    def send_first(c):
+        s = r.st[0, c]
+        r.mixfull[0, xi, c, core] = (s * norm_rows(s) * r.ngf[0, 0:1, :]).astype(BF16)
+        ag_start(0, r.mixfull.at[0], c)
+
+    loop(N, send_first)
+
+    r.grad[...] = mm(permutation(tokens), r.ct[...]).reshape(N, R, D)
+    first_grad = r.gfull.at[0]
+
+    def keep_cotangent(c):
+        first_grad[xi, c, core] = r.grad[c].astype(BF16)
+
+    loop(N, keep_cotangent)
     width = tokens // SEGS
-    row = iota((tokens, tokens), 0)
-    col = iota((tokens, tokens), 1)
-    place = lax.rem(row, SEGS) * width + row // SEGS
-    perm = jnp.where(col == place, 1.0, 0.0).astype(BF16)
-    r.st[0] = mm(perm, r.x[...]).reshape(N, R, D)
-    r.grad[...] = mm(perm, r.ct[...]).reshape(N, R, D)
-
-    r.ngf[...] = r.ng[...].astype(F32)
+    for k in range(5):
+        r.wmix[:, k * C + ch : (k + 1) * C, :] = jnp.zeros((L, C - ch, D), BF16)
+    for k in range(2):
+        r.wout[:, k * C + ch : (k + 1) * C, :] = jnp.zeros((L, C - ch, D), BF16)
     r.par[...] = jnp.zeros_like(r.par)
     r.gacc[...] = jnp.zeros_like(r.gacc)
     r.wg[:, z.units - 1, 1] = jnp.zeros((L, z.blk, D), BF16)
@@ -469,13 +633,10 @@
         def send_mix(c):
             @pl.when(l > 0)
             def _():
-                r.st[2 * l, c] = r.st[2 * l - 1, c] + rs_final(e - 1, r.ffnfull.at[l - 1], c)
-
-            s = r.st[2 * l, c]
-            full[xi, c, core] = (s * norm_rows(s) * r.ngf[l, 0:1, :]).astype(BF16)
-            ag_start(e, full, c)
-
-        loop(N, send_mix)
+                s = r.st[2 * l - 1, c] + rs_final(e - 1, r.ffnfull.at[l - 1], c)
+                r.st[2 * l, c] = s
+                full[xi, c, core] = (s * norm_rows(s) * r.ngf[l, 0:1, :]).astype(BF16)
+                ag_start(e, full, c)
 
         @pl.when(l == 0)
         def _():
@@ -496,7 +657,12 @@
             r.drive[1, chip, c] = ((1.0 - rate) * in_im * sigmoid(in_im)).reshape(2, R, C)
             scan_local(l, chip, c, turn_cos, turn_sin)
 
-        gather_loop(e, full, ascending, project)
+        exchange_loop(e, full, ascending, send_mix, project)
+
+        def send_cotangent(i):
+            ag_start(2 * L, first_grad, l * z.early + i)
+
+        loop(z.early, send_cotangent)
         r.segk[l] = r.seg[2]
         carry_over(l, False)
         for part in range(2):
@@ -523,20 +689,14 @@
             r.mixed[l, chip, c, :, :, C : 2 * C] = m_im.reshape(2, R, C)
             r.psc[...] = mm(flat(r.mixed[l, chip, c]), r.wout[l]).reshape(2, R, D)
 
-            @pl.when(j < N)
-            def _():
-                rs_other(e, c)
-
-            @pl.when((j >= 1) & (j <= N))
-            def _():
-                rs_pass(e, j - 1)
-
-            @pl.when(j >= N)
-            def _():
-                rs_own(e, c)
+            rs_step(e, j, ascending, False)
 
         loop(2 * N, mix)
 
+        def take_cotangent(i):
+            ag_take_x(2 * L, first_grad, l * z.early + i)
+
+        loop(z.early, take_cotangent)
         e2 = e + 1
         full2 = r.ffnfull.at[l]
 
@@ -545,8 +705,6 @@
             r.st[2 * l + 1, c] = s
             full2[xi, c, core] = (s * norm_rows(s) * r.ngf[l, 1:2, :]).astype(BF16)
             ag_start(e2, full2, c)
-
-        loop(N, send_ffn)
 
         def feed(j):
             chip, c = chip_chunk(j, ascending, True)
@@ -557,30 +715,17 @@
             r.hidden[l, chip, c] = hidden.reshape(2, R, F)
             r.psc[...] = mm(hidden, r.wdown[l]).reshape(2, R, D)
 
-            @pl.when(j < N)
-            def _():
-                rs_own(e2, c)
-
-            @pl.when(j >= N)
-            def _():
-                rs_other(e2, c)
-
-            @pl.when(j > N)
-            def _():
-                rs_pass(e2, j - N - 1)
-
-        gather_loop(e2, full2, ascending, feed)
+            rs_step(e2, j, ascending, True)
+
+        exchange_loop(e2, full2, ascending, send_ffn, feed)
         rs_pass(e2, N - 1)
 
     loop(L, forward_layer)
 
     def last_sum(c):
         e = 2 * L - 1
-        r.st[2 * L, c] = r.st[2 * L - 1, c] + rs_final(e, r.ffnfull.at[L - 1], c)
-
-    loop(N, last_sum)
-    unperm = perm
-    r.out[...] = mm_tn(unperm, r.st[2 * L].reshape(tokens, D).astype(BF16)).astype(BF16)
+        s = r.st[2 * L - 1, c] + rs_final(e, r.ffnfull.at[L - 1], c)
+        r.out[pl.ds(pl.multiple_of(c * R, R), R), :] = s.astype(BF16)
 
     def norm_back(l, which, c, grad_out):
         s = r.st[2 * l + which, c]
@@ -597,24 +742,17 @@
         e = 2 * L + 2 * step
         full = r.gfull.at[0]
 
-        def send_ffn(j):
-            c = descending(j)
-
+        early = step == 0
+
+        def send_ffn(c):
             @pl.when(step > 0)
             def _():
                 norm_back(l + 1, 0, c, rs_final(e - 1, r.gfull.at[1], c))
-
-            full[xi, c, core] = r.grad[c].astype(BF16)
-            ag_start(e, full, c)
-
-        loop(N, send_ffn)
-
-        @pl.when(step > 0)
-        def _():
-            tick((step - 1) * z.units + 7)
+                full[xi, c, core] = r.grad[c].astype(BF16)
+                ag_start(e, full, c)
 
         def feed_back(j):
-            chip, c = chip_chunk(j, descending, True)
+            chip, c = chip_chunk(j, descending, step > 0)
             g_hidden = mm_nt(flat(full[chip, c]), r.wdown[l])
             both = flat(r.gup[l, chip, c]).astype(F32)
             gate, up = both[:, 0:F], both[:, F : 2 * F]
@@ -625,40 +763,30 @@
             r.dgu[chip, c, :, :, F : 2 * F] = g_up.reshape(2, R, F)
             r.psc[...] = mm_nt(flat(r.dgu[chip, c]), r.wffn[l]).reshape(2, R, D)
 
-            @pl.when(j < N)
-            def _():
-                rs_own(e, c)
-
-            @pl.when(j >= N)
-            def _():
-                rs_other(e, c)
-
-            @pl.when(j > N)
-            def _():
-                rs_pass(e, descending(j - N - 1))
-
-            @pl.when((step > 0) & (lax.rem(j, N) == N // 2))
-            def _():
-                tick((step - 1) * z.units + 8 + j // N)
-
-        gather_loop(e, full, descending, feed_back)
-        rs_pass(e, 0)
+            rs_step(e, j, descending, step > 0)
+
+            @pl.when((step > 0) & (j == 2))
+            def _():
+                tick(step * z.units - 1)
+
+        exchange_loop(e, full, descending, send_ffn, feed_back, early)
+
+        @pl.when(step > 0)
+        def _():
+            rs_pass(e, 0)
+
+        @pl.when(step == 0)
+        def _():
+            loop(N, last_sum)
 
         def ffn_tile(i):
             cols = pl.ds(pl.multiple_of(i * F, LANES), F)
-
-            @pl.when(i == 0)
-            def _():
-                part = mm_tn(flat(r.hidden[l]), flat(full[...])).astype(BF16)
-                r.wg[l, 0 : z.fu] = part.reshape(z.fu, 2, z.blk, D)
-
-            @pl.when(i > 0)
-            def _():
-                cols = pl.ds(pl.multiple_of((i - 1) * F, LANES), F)
-                part = mm_tn(flat(r.ffnfull[l, :, :, :, :, cols]), flat(r.dgu[...])).astype(BF16)
-                r.wg[l, pl.ds(i * z.fu, z.fu)] = part.reshape(z.fu, 2, z.blk, D)
-
-        loop(1 + D // F, ffn_tile)
+            part = mm_tn(flat(r.ffnfull[l, :, :, :, :, cols]), flat(r.dgu[...])).astype(BF16)
+            r.wg[l, pl.ds(i * z.fu, z.fu)] = part.reshape(z.fu, 2, z.blk, D)
+
+        loop(D // F, ffn_tile)
+        part = mm_tn(flat(r.hidden[l]), flat(full[...])).astype(BF16)
+        r.wg[l, z.units - 4 - z.fu : z.units - 4] = part.reshape(z.fu, 2, z.blk, D)
         first_tick = step * z.units
         tick(first_tick)
 
@@ -667,14 +795,11 @@
         e2 = e + 1
         full2 = r.gfull.at[1]
 
-        def send_mix(j):
-            c = descending(j)
+        def send_mix(c):
             norm_back(l, 1, c, rs_final(e, full, c))
             full2[xi, c, core] = r.grad[c].astype(BF16)
             ag_start(e2, full2, c)
 
-        loop(N, send_mix)
-        tick(first_tick + 1)
         r.seg[0:2] = jnp.zeros((2, 2, 2, SEGS, C), F32)
 
         def mix_back(j):
@@ -700,11 +825,11 @@
             r.keep[chip, c] = (lower + (1.0 - lower) * sigmoid(pre)).reshape(2, R, C)
             scan_back_local(l, chip, c, turn_cos, turn_sin)
 
-            @pl.when(lax.rem(j, N) == N // 2)
-            def _():
-                tick(first_tick + 2 + j // N)
-
-        gather_loop(e2, full2, descending, mix_back)
+            @pl.when(lax.rem(j, 3) == 1)
+            def _():
+                tick(first_tick + 1 + j // 3)
+
+        exchange_loop(e2, full2, descending, send_mix, mix_back)
         carry_over(l, True)
 
         def scan_back(j):
@@ -732,23 +857,16 @@
             r.dproj[chip, c, :, :, 2 * C : 3 * C] = d_f.astype(BF16).reshape(2, R, C)
             r.psc[...] = mm(flat(r.dproj[chip, c]), r.wmix[l]).reshape(2, R, D)
 
-            @pl.when(j < N)
-            def _():
-                rs_other(e2, c)
-
-            @pl.when((j >= 1) & (j <= N))
-            def _():
-                rs_pass(e2, descending(j - 1))
-
-            @pl.when(j >= N)
-            def _():
-                rs_own(e2, c)
-
-            @pl.when(lax.rem(j, N) == N // 2)
-            def _():
-                tick(first_tick + 4 + j // N)
-
-        loop(2 * N, scan_back)
+            rs_step(e2, j, descending, False)
+
+            @pl.when(j == N)
+            def _():
+                loop(2, out_tile)
+                loop(2, gate_tile)
+
+            @pl.when((j == 2) | (j == 3) | (j == N) | (j == 2 * N - 1))
+            def _():
+                tick(first_tick + jnp.where(j == 2 * N - 1, 7, 2 + j))
 
         base_unit = z.units - 4
 
@@ -757,16 +875,20 @@
             part = mm_tn(flat(r.mixed[l, :, :, :, :, cols]), flat(full2[...])).astype(BF16)
             r.wg[l, base_unit, i] = part[0:ch]
 
-        loop(2, out_tile)
-
-        def mix_tile(i):
-            k = lax.rem(i + 3, 5)
+        def proj_tile(k, unit, block):
             cols = pl.ds(pl.multiple_of(k * C, LANES), C)
             part = mm_tn(flat(r.dproj[:, :, :, :, cols]), flat(r.mixfull[l])).astype(BF16)
-            r.wg[l, base_unit + 1 + i // 2, lax.rem(i, 2)] = part[0:ch]
-
-        loop(5, mix_tile)
-        tick(first_tick + 6)
+            r.wg[l, unit, block] = part[0:ch]
+
+        def gate_tile(i):
+            proj_tile(3 + i, base_unit + 1, i)
+
+        def in_tile(i):
+            proj_tile(i, base_unit + 2 + i // 2, lax.rem(i, 2))
+
+        loop(2 * N, scan_back)
+        loop(3, in_tile)
+        tick(first_tick + 8)
 
     loop(L, backward_layer)
 
@@ -775,7 +897,7 @@
         norm_back(0, 0, c, rs_final(4 * L - 1, r.gfull.at[1], c))
 
     loop(N, last_grad)
-    r.ig[...] = mm_tn(perm, r.grad[...].reshape(tokens, D).astype(BF16)).astype(BF16)
+    r.ig[...] = r.grad[...].reshape(tokens, D).astype(BF16)
 
     r.swork[...] = jnp.zeros_like(r.swork)
     for l in range(L):
@@ -783,14 +905,6 @@
             at = 2 * l + which
             r.swork[at : at + 1, :] = jnp.sum(r.gacc[l, which], axis=0, keepdims=True)
 
-    def swap_sum(k, peer, first):
-        copy = remote(r.swork, r.sland.at[k], r.ss.at[k], r.sr.at[k], peer)
-        copy.start()
-        copy.wait()
-        r.swork[...] = r.swork[...] + r.sland[k]
-
-    swap_sum(0, sib, True)
-    swap_sum(1, xnb, True)
     for l in range(L):
         for k in range(4):
             value = jnp.sum(r.sacc[l, k], axis=0, keepdims=True)
@@ -799,17 +913,78 @@
                 value = value * lower * (1.0 - lower)
             at = 2 * L + 4 * l + k
             r.swork[at : at + 1, 0:C] = value
-    if z.reduce:
-        swap_sum(2, y_peer, False)
-        swap_sum(3, pair_peer, False)
-        swap_sum(4, cross_peer, False)
-        start = (L - 1) * z.units + 7
-
-        def drain(i):
-            tick(start + i)
-
-        loop(z.units + 5 - 7, drain)
+
+    swap_peers = [sib, xnb] + ([y_peer, pair_peer, cross_peer] if z.reduce else [])
+    n_swaps = len(swap_peers)
+
+    def swap(k):
+        return remote(r.swork, r.sland.at[k], r.ss.at[k], r.sr.at[k], swap_peers[k])
+
+    def swap_step(i):
+        for k in range(n_swaps):
+
+            @pl.when(i == k + 1)
+            def _():
+                swap(k).wait()
+                rows = 2 * L if k < 2 else 2 * SEGS
+                r.swork[0:rows, :] = r.swork[0:rows, :] + r.sland[k, 0:rows, :]
+
+            @pl.when(i == k)
+            def _():
+                swap(k).start()
+
+    start = L * z.units - 1
+    ticks = 1 + 5 * LAG
+
+    def drain(i):
+        swap_step(i)
+        tick(start + i)
+
+    loop(ticks if z.reduce else n_swaps + 1, drain)
     r.sums[...] = r.swork[...]
+
+    def write_out(u):
+        if not z.reduce:
+            unit_out(u).start()
+        unit_out(u).wait()
+
+    loop(z.units * L, write_out)
+
+
+def finish(z, n_tensor, out, ig, sums, w_in, w_forget, w_gate, w_out, w_ffn, w_down, *o):
+    L, ch, F = z.L, z.ch, z.F
+    l, i = pl.program_id(0), pl.program_id(1)
+    tokens = out.shape[0]
+
+    @pl.when((l == 0) & (i == 0))
+    def _():
+        o[0][...] = mm_tn(permutation(tokens), out[...]).astype(BF16)
+        me = lax.axis_index("tensor")
+        piece = z.D // n_tensor
+        for t in range(n_tensor):
+
+            @pl.when(me == t)
+            def _():
+                for k in range(L):
+                    o[2][k] = sums[2 * k : 2 * k + 2, t * piece : (t + 1) * piece]
+
+        for k in range(L):
+            at = 2 * L + 4 * k
+            o[7][k : k + 1, :] = sums[at + 2 : at + 3, 0:ch]
+            o[8][k : k + 1, :] = sums[at + 3 : at + 4, 0:ch]
+            o[9][k] = sums[at : at + 2, 0:ch]
+
+    @pl.when((l == 0) & (i == 1))
+    def _():
+        o[1][...] = mm_tn(permutation(tokens), ig[...]).astype(BF16)
+
+    o[3][...] = w_in[...].astype(F32)
+    o[4][...] = w_forget[...].astype(F32)
+    o[5][...] = w_gate[...].astype(F32)
+    o[6][...] = w_out[...].astype(F32)
+    o[10][0, 0] = w_ffn[0, :, 0:F].astype(F32)
+    o[10][0, 1] = w_ffn[0, :, F : 2 * F].astype(F32)
+    o[11][...] = w_down[...].astype(F32)
 
 
 def local(*args):
@@ -825,11 +1000,13 @@
     z = types.SimpleNamespace(
         L=L, D=D, C=C, F=F, ch=ch, R=x.shape[0] // CHUNKS, reduce=reduce, blk=ch, fu=fu, units=units
     )
+    z.early = CHUNKS // L
     names, scratch = scratch_of(z)
     vmem = pl.BlockSpec(memory_space=pltpu.VMEM)
+    anywhere = pl.BlockSpec(memory_space=pl.ANY)
     in_specs = [vmem] * 12
     for k in (3, 4, 5, 6, 10, 11):
-        in_specs[k] = pl.BlockSpec(memory_space=pl.ANY)
+        in_specs[k] = anywhere
     shape = jax.ShapeDtypeStruct
     out, ig, wg, sums = pl.pallas_call(
         functools.partial(mega, z, names),
@@ -840,7 +1017,7 @@
             shape((2 * SEGS, D), F32),
         ),
         in_specs=in_specs,
-        out_specs=[vmem] * 4,
+        out_specs=[vmem, vmem, anywhere, vmem],
         scratch_shapes=scratch,
         compiler_params=pltpu.CompilerParams(
             collective_id=0, has_side_effects=True, vmem_limit_bytes=VMEM_BYTES
@@ -853,27 +1030,72 @@
     elif n_dp > 8:
         groups = [list(range(k, n_dp, 8)) for k in range(8)]
         wg, sums = lax.psum((wg, sums), "dp", axis_index_groups=groups)
-    wg = wg.astype(F32)
-    gains = sums[: 2 * L].reshape(L, 2, D)
-    piece = D // lax.axis_size("tensor")
-    gains = lax.dynamic_slice_in_dim(gains, lax.axis_index("tensor") * piece, piece, 2)
-    small = sums[2 * L : 6 * L, :ch].reshape(L, 4, ch)
-    g_down = wg[:, :fu].reshape(L, F, D)
-    g_ffn = wg[:, fu : units - 4].reshape(L, D, 2 * F)
-    return (
-        out,
-        ig,
-        gains,
-        jnp.swapaxes(wg[:, units - 2], 2, 3),
-        jnp.swapaxes(wg[:, units - 1, 0], 1, 2),
-        jnp.swapaxes(wg[:, units - 3], 2, 3),
-        wg[:, units - 4],
-        small[:, 2],
-        small[:, 3],
-        small[:, 0:2],
-        jnp.stack([g_ffn[:, :, :F], g_ffn[:, :, F:]], axis=1),
-        g_down,
-    )
+    n_tensor = lax.axis_size("tensor")
+    blocks = wg.reshape(L, 2 * units, ch, D)
+    rows = wg.reshape(L, 2 * units * ch, D)
+    G = 3
+    piece = ch // G
+
+    def block_spec(count, index):
+        return pl.BlockSpec((1, count, piece, D), lambda l, i: (l, index, i, 0))
+
+    def row_spec(size, index):
+        return pl.BlockSpec((1, size, D), lambda l, i: (l, index + i, 0))
+
+    def whole(*dims):
+        return pl.BlockSpec(dims, lambda l, i: (0,) * len(dims))
+
+    first = 2 * (units - 4)
+    res = pl.pallas_call(
+        functools.partial(finish, z, n_tensor),
+        grid=(L, G),
+        out_shape=(
+            shape(x.shape, BF16),
+            shape(x.shape, BF16),
+            shape((L, 2, D // n_tensor), F32),
+            shape((L, 2, ch, D), F32),
+            shape((L, 1, ch, D), F32),
+            shape((L, 2, ch, D), F32),
+            shape((L, 2, ch, D), F32),
+            shape((L, ch), F32),
+            shape((L, ch), F32),
+            shape((L, 2, ch), F32),
+            shape((L, 2, D, F), F32),
+            shape((L, F, D), F32),
+        ),
+        in_specs=[
+            whole(*x.shape),
+            whole(*x.shape),
+            whole(2 * SEGS, D),
+            block_spec(2, first // 2 + 2),
+            block_spec(1, first + 6),
+            block_spec(2, first // 2 + 1),
+            block_spec(2, first // 2),
+            row_spec(D // G, 0),
+            row_spec(F // G, D // (F // G)),
+        ],
+        out_specs=[
+            whole(*x.shape),
+            whole(*x.shape),
+            whole(L, 2, D // n_tensor),
+            block_spec(2, 0),
+            block_spec(1, 0),
+            block_spec(2, 0),
+            block_spec(2, 0),
+            whole(L, ch),
+            whole(L, ch),
+            whole(L, 2, ch),
+            pl.BlockSpec((1, 2, D // G, F), lambda l, i: (l, 0, i, 0)),
+            row_spec(F // G, 0),
+        ],
+        compiler_params=pltpu.CompilerParams(vmem_limit_bytes=VMEM_BYTES),
+        name="finish",
+    )(out, ig, sums, blocks, blocks, blocks, blocks, rows, rows)
+    res = list(res)
+    res[3] = jnp.swapaxes(res[3], 2, 3)
+    res[4] = jnp.swapaxes(res[4][:, 0], 1, 2)
+    res[5] = jnp.swapaxes(res[5], 2, 3)
+    return tuple(res)
 
 
 def solution(mesh):

time: 279 us -> 252 us (0.903)
  Pallas kernels: 262 us -> 251 us
  local copies, waits for them, and re-layouts: 9.94 us -> 0 us
  other arithmetic: 6.83 us -> 0 us
    pallas_call x1, Pallas kernels: 262 us -> 242 us  [local(): pl.pallas_call(functools.partial(mega, z, names), out_shape=(shape(x.shap...]
    pallas_call x0 -> x1, Pallas kernels: none -> 8.67 us  [local(): pl.pallas_call(functools.partial(finish, z, n_tensor), grid=(L, G), out_s...]
    slice x6 -> x0, local copies, waits for them, and re-layouts: 4.71 us -> none  [the longest x1 1.62 us: local(): g_down = wg[:, :fu].reshape(L, F, D)]
    convert_element_type x1 -> x0, other arithmetic: 4.34 us -> none  [local(): wg = wg.astype(F32)]
where the time goes in v3:
time: 252 us; the launch traced here: 251 us
  Pallas kernels  251 us (100%)
    pallas_call x1, Pallas kernels, local(): pl.pallas_call(functools.partial(mega, z, names), out_shape=(shape(x.shap...  242 us
    pallas_call x1, Pallas kernels, local(): pl.pallas_call(functools.partial(finish, z, n_tensor), grid=(L, G), out_s...  8.67 us

profile of v3, /device:TPU:0, one launch (start us, length us, event | category | flops | bytes accessed | tf_op | source)
XLA Modules:
  0.0 251.3 jit_solution(9901710894165308755)
XLA Ops:
  0.6 242.0 %layers.1 = (bf16[256,768]{1,0:T(8,128)(2,1)}, bf16[256,768]{1,0:T(8,128)(2,1)}, bf16[2,10,2,96,768]{4,3,2,1,0:T(8,128)(2,1)}, f32[16,768]{1,0:T(8,128)}) custom-call(bf16[256,768]{1,0:T(8,128)(2,1)} %refs_0_.1, bf16[256,768]{1,0:T(8,128)(2,1)} %refs_1_.1, bf16[2,2,768]{2,1,0:T(2,128)(2,1)} %refs_2_.1, bf16[2,2,96,768]{3,2,1,0:T(8,128)(2,1)} %bitcast.16, ...), custom_call_target="tpu_custom_call" | custom-call | tf_op jit(solution)/shard_map/layers/pallas_call | solution.py:1011
  242.6 8.7 %finish.1 = (bf16[256,768]{1,0:T(8,128)(2,1)}, bf16[256,768]{1,0:T(8,128)(2,1)}, f32[2,2,192]{2,1,0:T(2,128)}, f32[2,2,96,768]{3,2,1,0:T(8,128)}, f32[2,1,96,768...) custom-call(bf16[256,768]{1,0:T(8,128)(2,1)} %get-tuple-element.28.o, ...), custom_call_target="tpu_custom_call" | custom-call | tf_op jit(solution)/shard_map/finish/pallas_call | solution.py:1049

commit v4 on v3

--- a/solution.py
+++ b/solution.py
@@ -19,7 +19,11 @@
 SEGS = 8
 CHUNKS = 4
 LAG = 2
-UNIT_PIECES = 3
+PACE = (
+    dict(feed=(1, 0, 0, 1, 0, 0, 1, 0), feed_end=0, ffn_end=2, mix=(1, 0, 1, 0, 1, 1, 1, 1), scan=(0, 1, 0, 1, 1, 0, 1, 0), end=2),
+    dict(feed=(1, 0, 1, 0, 1, 0, 0, 1), feed_end=1, ffn_end=2, mix=(1, 0, 1, 0, 1, 1, 1, 1), scan=(0, 1, 0, 1, 1, 0, 1, 0), end=2),
+)
+AHEAD = 1
 PIECES = 2
 SLOTS = 10
 VMEM_BYTES = 63 * 1024 * 1024
@@ -104,9 +108,9 @@
         sland=((5, 2 * SEGS, D), F32),
     )
     if z.reduce:
-        unit = (SLOTS, z.blk, D)
+        unit = (SLOTS, z.sub, D)
         bufs.update(yland=(unit, BF16), mland=(unit, BF16))
-        bufs.update(zland=((SLOTS // 2, z.blk, D), BF16), zfold=((SLOTS // 2, 2, z.blk, D), BF16))
+        bufs.update(zland=(unit, BF16), zfold=((SLOTS, 2, z.sub, D), BF16))
     sems = dict(
         ags=(4 * L, 3, N),
         agr=(4 * L, 3, N),
@@ -115,10 +119,10 @@
         wsem=(L, 10),
         ss=(5,),
         sr=(5,),
-        outs=(z.units * L,),
+        outs=(z.period * L,),
     )
     if z.reduce:
-        sems.update(us=(z.units * L, 5), ur=(z.units * L, 5))
+        sems.update(us=(z.period * L, 5), ur=(z.period * L, 5))
     names = list(bufs) + list(sems)
     shapes = [pltpu.VMEM(s, d) for s, d in bufs.values()]
     shapes += [pltpu.SemaphoreType.DMA(s) for s in sems.values()]
@@ -187,45 +191,54 @@
                     else:
                         copy(src.at[at], dst.at[at]).start()
 
-        whole = copy(src, dst)
         return types.SimpleNamespace(
-            start=start, wait_recv=whole.wait_recv, wait_send=whole.wait_send, wait=whole.wait
+            start=start,
+            wait_recv=lambda: copy(src, dst).wait_recv(),
+            wait_send=lambda: copy(src, dst).wait_send(),
+            wait=lambda: copy(src, dst).wait(),
         )
 
+    n_ffn = z.units - 4
+    period = z.period
+
     def unit_of(u):
-        return L - 1 - u // z.units, lax.rem(u, z.units)
+        s = u % period
+        k = s // 2
+        k = (k + n_ffn - z.fu) % n_ffn if k < n_ffn else k
+        return L - 1 - u // period, k, slice((s % 2) * z.sub, (s % 2 + 1) * z.sub)
 
     half = line // 2
 
     def unit_copy(u, stage, even):
-        l, k = unit_of(u)
-        slot = lax.rem(u, SLOTS)
-        mine = r.wg.at[l, k, y]
+        l, k, rows = unit_of(u)
+        slot = u % SLOTS
+        both = r.wg.at[l, k, :, rows]
         if even:
-            part = r.wg.at[l, k, half]
+            part = r.wg.at[l, k, half, rows]
             src, dst, peer = (
-                (r.wg.at[l, k], r.zfold.at[slot // 2], pair_peer),
-                (r.wg.at[l, k, 1 - half], r.mland.at[slot], cross_peer),
+                (both, r.zfold.at[slot], pair_peer),
+                (r.wg.at[l, k, 1 - half, rows], r.mland.at[slot], cross_peer),
                 (part, r.yland.at[slot], y_peer),
                 (part, part, cross_peer),
-                (r.wg.at[l, k], r.wg.at[l, k], pair_peer),
+                (both, both, pair_peer),
             )[stage]
         else:
+            mine = r.wg.at[l, k, y, rows]
             src, dst, peer = (
-                (r.wg.at[l, k, 1 - y], r.yland.at[slot], y_peer),
-                (mine, r.zland.at[slot // 2], pair_peer),
+                (r.wg.at[l, k, 1 - y, rows], r.yland.at[slot], y_peer),
+                (mine, r.zland.at[slot], pair_peer),
                 (mine, r.mland.at[slot], cross_peer),
-                (mine, r.zland.at[slot // 2], pair_peer),
+                (mine, r.zland.at[slot], pair_peer),
                 (mine, mine, y_peer),
             )[stage]
-        return remote(src, dst, r.us.at[u, stage], r.ur.at[u, stage], peer, UNIT_PIECES)
+        return remote(src, dst, r.us.at[u, stage], r.ur.at[u, stage], peer)
 
     def unit_land(u, stage, ref, peer):
         return remote(ref, ref, r.us.at[u, stage], r.ur.at[u, stage], peer)
 
     def unit_add(u, part, landed):
-        l, k = unit_of(u)
-        r.wg[l, k, part] = (r.wg[l, k, part].astype(F32) + landed.astype(F32)).astype(BF16)
+        l, k, rows = unit_of(u)
+        r.wg[l, k, part, rows] = (r.wg[l, k, part, rows].astype(F32) + landed.astype(F32)).astype(BF16)
 
     def tell(sem, peer):
         pl.semaphore_signal(sem, inc=1, device_id=peer, device_id_type=MESH)
@@ -238,8 +251,8 @@
 
     def odd_stage(u, stage):
         copy = lambda n: unit_copy(u, n, False)
-        slot = lax.rem(u, SLOTS)
-        l, k = unit_of(u)
+        slot = u % SLOTS
+        l, k, rows = unit_of(u)
         if stage == 0:
             copy(0).start()
         if stage == 1:
@@ -253,7 +266,7 @@
             @on_middle
             def _():
                 copy(1).wait_recv()
-                unit_add(u, y, r.zland[slot // 2])
+                unit_add(u, y, r.zland[slot])
                 copy(2).start()
 
         if stage == 3:
@@ -271,20 +284,20 @@
             def _():
                 copy(1).wait_send()
                 copy(3).wait_recv()
-                r.wg[l, k, y] = r.zland[slot // 2]
+                r.wg[l, k, y, rows] = r.zland[slot]
 
             pl.semaphore_wait(r.freed.at[0], 1)
             copy(4).start()
         if stage == 5:
-            unit_land(u, 4, r.wg.at[l, k, 1 - y], y_peer).wait_recv()
+            unit_land(u, 4, r.wg.at[l, k, 1 - y, rows], y_peer).wait_recv()
             copy(4).wait_send()
             on_middle(lambda: copy(3).wait_send())
             unit_out(u).start()
 
     def even_stage(u, stage):
         copy = lambda n: unit_copy(u, n, True)
-        slot = lax.rem(u, SLOTS)
-        l, k = unit_of(u)
+        slot = u % SLOTS
+        l, k, rows = unit_of(u)
         if stage == 0:
             on_end(lambda: copy(0).start())
         if stage == 1:
@@ -298,7 +311,7 @@
             def _():
                 copy(0).wait_recv()
                 for part in range(2):
-                    unit_add(u, part, r.zfold[slot // 2, part])
+                    unit_add(u, part, r.zfold[slot, part])
                 copy(1).start()
 
         if stage == 2:
@@ -325,7 +338,7 @@
 
             @on_middle
             def _():
-                unit_land(u, 3, r.wg.at[l, k, 1 - half], cross_peer).wait_recv()
+                unit_land(u, 3, r.wg.at[l, k, 1 - half, rows], cross_peer).wait_recv()
                 pl.semaphore_wait(r.freed.at[1], 1)
                 copy(4).start()
 
@@ -340,24 +353,30 @@
             unit_out(u).start()
 
     def unit_out(u):
-        l, k = unit_of(u)
-        return pltpu.make_async_copy(r.wg.at[l, k], r.wgout.at[l, k], r.outs.at[u])
-
-    def tick(m):
-        if not z.reduce:
-            return
-        for stage in reversed(range(6)):
-            u = m - LAG * stage
-
-            there = (u >= 0) & (u < z.units * L)
-
-            @pl.when(there & (lax.rem(u, 2) == 1))
-            def _():
-                odd_stage(u, stage)
-
-            @pl.when(there & (lax.rem(u, 2) == 0))
-            def _():
-                even_stage(u, stage)
+        l, k, rows = unit_of(u)
+        return pltpu.make_async_copy(r.wg.at[l, k, :, rows], r.wgout.at[l, k, :, rows], r.outs.at[u])
+
+    clock = [0]
+    last_tick = period * L + 5 * LAG
+
+    def ticks(count, ready=None):
+        for _ in range(count if z.reduce else 0):
+            m = clock[0]
+            if m >= last_tick or (ready is not None and m >= ready):
+                return
+            clock[0] = m + 1
+            for stage in reversed(range(6)):
+                u = m - LAG * stage
+                if 0 <= u < period * L:
+                    (even_stage if u % 2 == 0 else odd_stage)(u, stage)
+
+    def ticks_in_loop(i, counts, ready):
+        for at, count in enumerate(counts):
+            if count:
+
+                @pl.when(i == at)
+                def _():
+                    ticks(count, ready(at))
 
     def ag_copy(e, full, c, kind):
         chip = other if kind == 2 else xi
@@ -417,38 +436,35 @@
             ag_copy(e, full, c, kind).wait_send()
         return total
 
-    def exchange_loop(e, full, order, send, stage, early=None):
-        def when_late(cond, body):
-            pl.when(cond if early is None else cond & jnp.logical_not(early))(body)
-
+    def exchange_loop(e, full, order, send, stage, early=False):
         send(order(0))
-        if early is not None:
-
-            @pl.when(early)
-            def _():
-                def take(c):
-                    ag_landing(e, full, c, 1).wait_recv()
-                    ag_landing(e, full, c, 2).wait_recv()
-
-                loop(N, take)
+        if early:
+
+            def take(c):
+                ag_landing(e, full, c, 1).wait_recv()
+                ag_landing(e, full, c, 2).wait_recv()
+
+            loop(N, take)
 
         def step(i):
             @pl.when(i + 1 < N)
             def _():
                 send(order(i + 1))
 
-            def take_sib():
-                ag_landing(e, full, order(i), 1).wait_recv()
-
-            def take_x():
-                ag_take_x(e, full, order(i - N + 1))
-
-            def take_far():
-                ag_landing(e, full, order(i - N), 2).wait_recv()
-
-            when_late(i < N, take_sib)
-            when_late((i >= N - 1) & (i < 2 * N - 1), take_x)
-            when_late(i >= N, take_far)
+            if not early:
+
+                @pl.when(i < N)
+                def _():
+                    ag_landing(e, full, order(i), 1).wait_recv()
+
+                @pl.when((i >= N - 1) & (i < 2 * N - 1))
+                def _():
+                    ag_take_x(e, full, order(i - N + 1))
+
+                @pl.when(i >= N)
+                def _():
+                    ag_landing(e, full, order(i - N), 2).wait_recv()
+
             stage(i)
 
         loop(2 * N, step)
@@ -456,21 +472,21 @@
     def chip_chunk(i, order, own_first):
         first = i < N
         chunk = order(jnp.where(first, i, i - N))
-        return jnp.where(first == own_first, xi, other), chunk
+        return jnp.where(first, xi, other) if own_first else jnp.where(first, other, xi), chunk
 
     def rs_step(e, i, order, own_first):
         first = i < N
         chunk = order(jnp.where(first, i, i - N))
 
-        @pl.when(first == own_first)
+        @pl.when(first if own_first else i >= N)
         def _():
             rs_own(e, chunk)
 
-        @pl.when(first != own_first)
+        @pl.when(i >= N if own_first else first)
         def _():
             rs_other(e, chunk)
 
-        behind = jnp.where(own_first, i - N, i) - 1
+        behind = (i - N if own_first else i) - 1
 
         @pl.when((behind >= 0) & (behind < N))
         def _():
@@ -532,7 +548,6 @@
         r.wout[:, k * C + ch : (k + 1) * C, :] = jnp.zeros((L, C - ch, D), BF16)
     r.par[...] = jnp.zeros_like(r.par)
     r.gacc[...] = jnp.zeros_like(r.gacc)
-    r.wg[:, z.units - 1, 1] = jnp.zeros((L, z.blk, D), BF16)
     r.sacc[...] = jnp.zeros_like(r.sacc)
     for l in range(L):
         angle = r.ph[l : l + 1, :]
@@ -742,11 +757,11 @@
         e = 2 * L + 2 * step
         full = r.gfull.at[0]
 
-        early = step == 0
+        base = step * period
+        pace = PACE[min(step, 1)]
 
         def send_ffn(c):
-            @pl.when(step > 0)
-            def _():
+            if step > 0:
                 norm_back(l + 1, 0, c, rs_final(e - 1, r.gfull.at[1], c))
                 full[xi, c, core] = r.grad[c].astype(BF16)
                 ag_start(e, full, c)
@@ -765,18 +780,17 @@
 
             rs_step(e, j, descending, step > 0)
 
-            @pl.when((step > 0) & (j == 2))
-            def _():
-                tick(step * z.units - 1)
-
-        exchange_loop(e, full, descending, send_ffn, feed_back, early)
-
-        @pl.when(step > 0)
-        def _():
+            @pl.when(j == (2 * N - 1 if step > 0 else 0))
+            def _():
+                part = mm_tn(flat(r.hidden[l]), flat(full[...])).astype(BF16)
+                r.wg[l, n_ffn - z.fu : n_ffn] = part.reshape(z.fu, 2, z.blk, D)
+
+            ticks_in_loop(j, pace["feed"], lambda at: base + (4 if step == 0 or at == 2 * N - 1 else 0))
+
+        exchange_loop(e, full, descending, send_ffn, feed_back, step == 0)
+        if step > 0:
             rs_pass(e, 0)
-
-        @pl.when(step == 0)
-        def _():
+        else:
             loop(N, last_sum)
 
         def ffn_tile(i):
@@ -784,11 +798,9 @@
             part = mm_tn(flat(r.ffnfull[l, :, :, :, :, cols]), flat(r.dgu[...])).astype(BF16)
             r.wg[l, pl.ds(i * z.fu, z.fu)] = part.reshape(z.fu, 2, z.blk, D)
 
+        ticks(pace["feed_end"], base + 4)
         loop(D // F, ffn_tile)
-        part = mm_tn(flat(r.hidden[l]), flat(full[...])).astype(BF16)
-        r.wg[l, z.units - 4 - z.fu : z.units - 4] = part.reshape(z.fu, 2, z.blk, D)
-        first_tick = step * z.units
-        tick(first_tick)
+        ticks(pace["ffn_end"], base + 12)
 
         turn_cos, turn_sin, lower = r.par[l, 0:1, :], r.par[l, 1:2, :], r.par[l, 2:3, :]
         gain_re, gain_im = r.par[l, 3:4, :], r.par[l, 4:5, :]
@@ -825,9 +837,7 @@
             r.keep[chip, c] = (lower + (1.0 - lower) * sigmoid(pre)).reshape(2, R, C)
             scan_back_local(l, chip, c, turn_cos, turn_sin)
 
-            @pl.when(lax.rem(j, 3) == 1)
-            def _():
-                tick(first_tick + 1 + j // 3)
+            ticks_in_loop(j, pace["mix"], lambda at: base + 12)
 
         exchange_loop(e2, full2, descending, send_mix, mix_back)
         carry_over(l, True)
@@ -864,9 +874,7 @@
                 loop(2, out_tile)
                 loop(2, gate_tile)
 
-            @pl.when((j == 2) | (j == 3) | (j == N) | (j == 2 * N - 1))
-            def _():
-                tick(first_tick + jnp.where(j == 2 * N - 1, 7, 2 + j))
+            ticks_in_loop(j, pace["scan"], lambda at: base + (12 if at < N else 16))
 
         base_unit = z.units - 4
 
@@ -884,18 +892,26 @@
             proj_tile(3 + i, base_unit + 1, i)
 
         def in_tile(i):
-            proj_tile(i, base_unit + 2 + i // 2, lax.rem(i, 2))
+            proj_tile(i, base_unit + 2, i)
+
+        def forget_tile():
+            part = mm_tn(flat(r.dproj[:, :, :, :, 2 * C : 3 * C]), flat(r.mixfull[l])).astype(BF16)
+            for half in range(2):
+                r.wg[l, base_unit + 3, half, 0 : z.sub] = part[half * z.sub : (half + 1) * z.sub]
 
         loop(2 * N, scan_back)
-        loop(3, in_tile)
-        tick(first_tick + 8)
-
-    loop(L, backward_layer)
+        loop(2, in_tile)
+        forget_tile()
+        ticks(pace["end"], base + period)
+
+    for step in range(L):
+        backward_layer(step)
 
     def last_grad(j):
         c = descending(j)
         norm_back(0, 0, c, rs_final(4 * L - 1, r.gfull.at[1], c))
 
+    ticks(AHEAD)
     loop(N, last_grad)
     r.ig[...] = r.grad[...].reshape(tokens, D).astype(BF16)
 
@@ -920,35 +936,21 @@
     def swap(k):
         return remote(r.swork, r.sland.at[k], r.ss.at[k], r.sr.at[k], swap_peers[k])
 
-    def swap_step(i):
-        for k in range(n_swaps):
-
-            @pl.when(i == k + 1)
-            def _():
-                swap(k).wait()
-                rows = 2 * L if k < 2 else 2 * SEGS
-                r.swork[0:rows, :] = r.swork[0:rows, :] + r.sland[k, 0:rows, :]
-
-            @pl.when(i == k)
-            def _():
-                swap(k).start()
-
-    start = L * z.units - 1
-    ticks = 1 + 5 * LAG
-
-    def drain(i):
-        swap_step(i)
-        tick(start + i)
-
-    loop(ticks if z.reduce else n_swaps + 1, drain)
+    for i in range(max(n_swaps + 1, last_tick - clock[0])):
+        if 1 <= i <= n_swaps:
+            k = i - 1
+            swap(k).wait()
+            rows = 2 * L if k < 2 else 2 * SEGS
+            r.swork[0:rows, :] = r.swork[0:rows, :] + r.sland[k, 0:rows, :]
+        if i < n_swaps:
+            swap(i).start()
+        ticks(1)
     r.sums[...] = r.swork[...]
 
-    def write_out(u):
+    for u in range(period * L):
         if not z.reduce:
             unit_out(u).start()
         unit_out(u).wait()
-
-    loop(z.units * L, write_out)
 
 
 def finish(z, n_tensor, out, ig, sums, w_in, w_forget, w_gate, w_out, w_ffn, w_down, *o):
@@ -997,8 +999,10 @@
     reduce = n_dp % 8 == 0
     fu = F // (2 * ch)
     units = fu * (1 + D // F) + 4
+    sub = ch // 2
+    period = 2 * units - 1
     z = types.SimpleNamespace(
-        L=L, D=D, C=C, F=F, ch=ch, R=x.shape[0] // CHUNKS, reduce=reduce, blk=ch, fu=fu, units=units
+        L=L, D=D, C=C, F=F, ch=ch, R=x.shape[0] // CHUNKS, reduce=reduce, blk=ch, fu=fu, units=units, sub=sub, period=period
     )
     z.early = CHUNKS // L
     names, scratch = scratch_of(z)
@@ -1039,6 +1043,9 @@
     def block_spec(count, index):
         return pl.BlockSpec((1, count, piece, D), lambda l, i: (l, index, i, 0))
 
+    def part_spec(index):
+        return pl.BlockSpec((1, 2, sub // G, D), lambda l, i: (l, index, i, 0))
+
     def row_spec(size, index):
         return pl.BlockSpec((1, size, D), lambda l, i: (l, index + i, 0))
 
@@ -1054,7 +1061,7 @@
             shape(x.shape, BF16),
             shape((L, 2, D // n_tensor), F32),
             shape((L, 2, ch, D), F32),
-            shape((L, 1, ch, D), F32),
+            shape((L, 2, sub, D), F32),
             shape((L, 2, ch, D), F32),
             shape((L, 2, ch, D), F32),
             shape((L, ch), F32),
@@ -1068,7 +1075,7 @@
             whole(*x.shape),
             whole(2 * SEGS, D),
             block_spec(2, first // 2 + 2),
-            block_spec(1, first + 6),
+            part_spec(first // 2 + 3),
             block_spec(2, first // 2 + 1),
             block_spec(2, first // 2),
             row_spec(D // G, 0),
@@ -1079,7 +1086,7 @@
             whole(*x.shape),
             whole(L, 2, D // n_tensor),
             block_spec(2, 0),
-            block_spec(1, 0),
+            part_spec(0),
             block_spec(2, 0),
             block_spec(2, 0),
             whole(L, ch),
@@ -1093,7 +1100,7 @@
     )(out, ig, sums, blocks, blocks, blocks, blocks, rows, rows)
     res = list(res)
     res[3] = jnp.swapaxes(res[3], 2, 3)
-    res[4] = jnp.swapaxes(res[4][:, 0], 1, 2)
+    res[4] = jnp.swapaxes(res[4].reshape(L, ch, D), 1, 2)
     res[5] = jnp.swapaxes(res[5], 2, 3)
     return tuple(res)
 

time: 252 us -> 229 us (0.909)
  Pallas kernels: 251 us -> 227 us
    pallas_call x1, Pallas kernels: 242 us -> 219 us  [local(): pl.pallas_call(functools.partial(mega, z, names), out_shape=(shape(x.shap...]
where the time goes in v4:
time: 229 us; the launch traced here: 228 us
  Pallas kernels  227 us (99%)
    pallas_call x1, Pallas kernels, local(): pl.pallas_call(functools.partial(mega, z, names), out_shape=(shape(x.shap...  219 us
    pallas_call x1, Pallas kernels, local(): pl.pallas_call(functools.partial(finish, z, n_tensor), grid=(L, G), out_s...  8.67 us

profile of v4, /device:TPU:0, one launch (start us, length us, event | category | flops | bytes accessed | tf_op | source)
XLA Modules:
  0.0 228.3 jit_solution(2448905538424937725)
XLA Ops:
  0.6 218.8 %layers.1 = (bf16[256,768]{1,0:T(8,128)(2,1)}, bf16[256,768]{1,0:T(8,128)(2,1)}, bf16[2,10,2,96,768]{4,3,2,1,0:T(8,128)(2,1)}, f32[16,768]{1,0:T(8,128)}) custom-call(bf16[256,768]{1,0:T(8,128)(2,1)} %refs_0_.1, bf16[256,768]{1,0:T(8,128)(2,1)} %refs_1_.1, bf16[2,2,768]{2,1,0:T(2,128)(2,1)} %refs_2_.1, bf16[2,2,96,768]{3,2,1,0:T(8,128)(2,1)} %bitcast.16, ...), custom_call_target="tpu_custom_call" | custom-call | tf_op jit(solution)/shard_map/layers/pallas_call | solution.py:1015
  219.5 8.7 %finish.1 = (bf16[256,768]{1,0:T(8,128)(2,1)}, bf16[256,768]{1,0:T(8,128)(2,1)}, f32[2,2,192]{2,1,0:T(2,128)}, f32[2,2,96,768]{3,2,1,0:T(8,128)}, f32[2,2,48,768...) custom-call(bf16[256,768]{1,0:T(8,128)(2,1)} %get-tuple-element.28.o, ...), custom_call_target="tpu_custom_call" | custom-call | tf_op jit(solution)/shard_map/finish/pallas_call | solution.py:1056

commit v5 on v4

--- a/solution.py
+++ b/solution.py
@@ -20,10 +20,10 @@
 CHUNKS = 4
 LAG = 2
 PACE = (
-    dict(feed=(1, 0, 0, 1, 0, 0, 1, 0), feed_end=0, ffn_end=2, mix=(1, 0, 1, 0, 1, 1, 1, 1), scan=(0, 1, 0, 1, 1, 0, 1, 0), end=2),
+    dict(feed=(1, 0, 0, 0, 1, 0, 0, 1), feed_end=0, ffn_end=1, mix=(1, 0, 1, 0, 1, 1, 1, 1), scan=(0, 1, 0, 1, 1, 0, 1, 0), end=2),
     dict(feed=(1, 0, 1, 0, 1, 0, 0, 1), feed_end=1, ffn_end=2, mix=(1, 0, 1, 0, 1, 1, 1, 1), scan=(0, 1, 0, 1, 1, 0, 1, 0), end=2),
 )
-AHEAD = 1
+AHEAD = 4
 PIECES = 2
 SLOTS = 10
 VMEM_BYTES = 63 * 1024 * 1024
@@ -95,7 +95,7 @@
         dgu=((*rows, 2 * F), BF16),
         dproj=((*rows, 5 * C), BF16),
         psc=((2, R, D), F32),
-        xpart=((*own, D), F32),
+        xpart=((2, *own, D), F32),
         opart=((2, *own, D), F32),
         grad=((*own, D), F32),
         stage=((2, 3, *own, D), BF16),
@@ -167,7 +167,6 @@
     barrier = pltpu.get_barrier_semaphore()
     for peer in peers:
         pl.semaphore_signal(barrier, inc=1, device_id=peer, device_id_type=MESH)
-    pl.semaphore_wait(barrier, len(peers))
 
     def remote(src, dst, send, recv, peer, pieces=1):
         def copy(source, target):
@@ -414,11 +413,11 @@
     def rs_other(e, c):
         r.stage[r_side(e), 0, c] = r.psc[1 - core].astype(BF16)
         rs_copy(e, c, 0).start()
-        r.xpart[c] = r.psc[core]
+        r.xpart[r_side(e), c] = r.psc[core]
 
     def rs_pass(e, c):
         rs_copy(e, c, 0).wait_recv()
-        r.stage[r_side(e), 1, c] = (r.xpart[c] + r.land[r_side(e), 0, c].astype(F32)).astype(BF16)
+        r.stage[r_side(e), 1, c] = (r.xpart[r_side(e), c] + r.land[r_side(e), 0, c].astype(F32)).astype(BF16)
         rs_copy(e, c, 1).start()
 
     def rs_own(e, c):
@@ -474,7 +473,7 @@
         chunk = order(jnp.where(first, i, i - N))
         return jnp.where(first, xi, other) if own_first else jnp.where(first, other, xi), chunk
 
-    def rs_step(e, i, order, own_first):
+    def rs_step(e, i, order, own_first, go=True):
         first = i < N
         chunk = order(jnp.where(first, i, i - N))
 
@@ -488,7 +487,7 @@
 
         behind = (i - N if own_first else i) - 1
 
-        @pl.when((behind >= 0) & (behind < N))
+        @pl.when((behind >= 0) & (behind < N) & go)
         def _():
             rs_pass(e, order(behind))
 
@@ -527,12 +526,13 @@
     r.st[0] = mm(permutation(tokens), r.x[...]).reshape(N, R, D)
     r.ngf[...] = r.ng[...].astype(F32)
 
-    def send_first(c):
+    def norm_first(c):
         s = r.st[0, c]
         r.mixfull[0, xi, c, core] = (s * norm_rows(s) * r.ngf[0, 0:1, :]).astype(BF16)
-        ag_start(0, r.mixfull.at[0], c)
-
-    loop(N, send_first)
+
+    loop(N, norm_first)
+    pl.semaphore_wait(barrier, len(peers))
+    loop(N, lambda c: ag_start(0, r.mixfull.at[0], c))
 
     r.grad[...] = mm(permutation(tokens), r.ct[...]).reshape(N, R, D)
     first_grad = r.gfull.at[0]
@@ -730,10 +730,13 @@
             r.hidden[l, chip, c] = hidden.reshape(2, R, F)
             r.psc[...] = mm(hidden, r.wdown[l]).reshape(2, R, D)
 
-            rs_step(e2, j, ascending, True)
+            rs_step(e2, j, ascending, True, l < L - 1)
 
         exchange_loop(e2, full2, ascending, send_ffn, feed)
-        rs_pass(e2, N - 1)
+
+        @pl.when(l < L - 1)
+        def _():
+            rs_pass(e2, N - 1)
 
     loop(L, forward_layer)
 
@@ -790,8 +793,6 @@
         exchange_loop(e, full, descending, send_ffn, feed_back, step == 0)
         if step > 0:
             rs_pass(e, 0)
-        else:
-            loop(N, last_sum)
 
         def ffn_tile(i):
             cols = pl.ds(pl.multiple_of(i * F, LANES), F)
@@ -902,6 +903,8 @@
         loop(2 * N, scan_back)
         loop(2, in_tile)
         forget_tile()
+        if step == L - 1:
+            loop(N, lambda c: rs_pass(2 * L - 1, c))
         ticks(pace["end"], base + period)
 
     for step in range(L):
@@ -945,6 +948,7 @@
         if i < n_swaps:
             swap(i).start()
         ticks(1)
+    loop(N, last_sum)
     r.sums[...] = r.swork[...]
 
     for u in range(period * L):
@@ -976,7 +980,7 @@
             o[8][k : k + 1, :] = sums[at + 3 : at + 4, 0:ch]
             o[9][k] = sums[at : at + 2, 0:ch]
 
-    @pl.when((l == 0) & (i == 1))
+    @pl.when((l == L - 1) & (i == 0))
     def _():
         o[1][...] = mm_tn(permutation(tokens), ig[...]).astype(BF16)
 
@@ -1037,7 +1041,7 @@
     n_tensor = lax.axis_size("tensor")
     blocks = wg.reshape(L, 2 * units, ch, D)
     rows = wg.reshape(L, 2 * units * ch, D)
-    G = 3
+    G = 1
     piece = ch // G
 
     def block_spec(count, index):

time: 229 us -> 225 us (0.983)
  Pallas kernels: 227 us -> 224 us
where the time goes in v5:
time: 225 us
  Pallas kernels  224 us (100%)
    pallas_call x1, Pallas kernels, local(): pl.pallas_call(functools.partial(mega, z, names), out_shape=(shape(x.shap...  217 us
    pallas_call x1, Pallas kernels, local(): pl.pallas_call(functools.partial(finish, z, n_tensor), grid=(L, G), out_s...  7.04 us

profile of v5, /device:TPU:0, one launch (start us, length us, event | category | flops | bytes accessed | tf_op | source)
XLA Modules:
  0.0 224.7 jit_solution(14656020264174099763)
XLA Ops:
  0.6 216.9 %layers.1 = (bf16[256,768]{1,0:T(8,128)(2,1)}, bf16[256,768]{1,0:T(8,128)(2,1)}, bf16[2,10,2,96,768]{4,3,2,1,0:T(8,128)(2,1)}, f32[16,768]{1,0:T(8,128)}) custom-call(bf16[256,768]{1,0:T(8,128)(2,1)} %refs_0_.1, bf16[256,768]{1,0:T(8,128)(2,1)} %refs_1_.1, bf16[2,2,768]{2,1,0:T(2,128)(2,1)} %refs_2_.1, bf16[2,2,96,768]{3,2,1,0:T(8,128)(2,1)} %bitcast.16, ...), custom_call_target="tpu_custom_call" | custom-call | tf_op jit(solution)/shard_map/layers/pallas_call | solution.py:1019
  217.5 7.0 %finish.1 = (bf16[256,768]{1,0:T(8,128)(2,1)}, bf16[256,768]{1,0:T(8,128)(2,1)}, f32[2,2,192]{2,1,0:T(2,128)}, f32[2,2,96,768]{3,2,1,0:T(8,128)}, f32[2,2,48,768...) custom-call(bf16[256,768]{1,0:T(8,128)(2,1)} %get-tuple-element.28.o, ...), custom_call_target="tpu_custom_call" | custom-call | tf_op jit(solution)/shard_map/finish/pallas_call | solution.py:1060

commit v6 on v5

--- a/solution.py
+++ b/solution.py
@@ -20,10 +20,10 @@
 CHUNKS = 4
 LAG = 2
 PACE = (
-    dict(feed=(1, 0, 0, 0, 1, 0, 0, 1), feed_end=0, ffn_end=1, mix=(1, 0, 1, 0, 1, 1, 1, 1), scan=(0, 1, 0, 1, 1, 0, 1, 0), end=2),
-    dict(feed=(1, 0, 1, 0, 1, 0, 0, 1), feed_end=1, ffn_end=2, mix=(1, 0, 1, 0, 1, 1, 1, 1), scan=(0, 1, 0, 1, 1, 0, 1, 0), end=2),
+    dict(feed=(1, 0, 0, 0, 1, 0, 0, 1), feed_end=0, ffn_end=1, mix=(1, 0, 1, 0, 1, 1, 1, 1), scan=(0, 0, 1, 1, 0, 1, 1, 0), end=1),
+    dict(feed=(1, 1, 1, 0, 1, 0, 0, 1), feed_end=1, ffn_end=2, mix=(1, 0, 1, 0, 1, 1, 1, 1), scan=(0, 1, 0, 1, 1, 0, 1, 0), end=2),
 )
-AHEAD = 4
+AHEAD = 6
 PIECES = 2
 SLOTS = 10
 VMEM_BYTES = 63 * 1024 * 1024
@@ -903,9 +903,9 @@
         loop(2 * N, scan_back)
         loop(2, in_tile)
         forget_tile()
+        ticks(pace["end"], base + period)
         if step == L - 1:
             loop(N, lambda c: rs_pass(2 * L - 1, c))
-        ticks(pace["end"], base + period)
 
     for step in range(L):
         backward_layer(step)

time: 225 us -> 223 us (level)
  no operation moved by 1% of the time
where the time goes in v6:
time: 223 us; the launch traced here: 222 us
  Pallas kernels  222 us (100%)
    pallas_call x1, Pallas kernels, local(): pl.pallas_call(functools.partial(mega, z, names), out_shape=(shape(x.shap...  215 us
    pallas_call x1, Pallas kernels, local(): pl.pallas_call(functools.partial(finish, z, n_tensor), grid=(L, G), out_s...  7.04 us

profile of v6, /device:TPU:0, one launch (start us, length us, event | category | flops | bytes accessed | tf_op | source)
XLA Modules:
  0.0 222.5 jit_solution(13616001322271979631)
XLA Ops:
  0.6 214.6 %layers.1 = (bf16[256,768]{1,0:T(8,128)(2,1)}, bf16[256,768]{1,0:T(8,128)(2,1)}, bf16[2,10,2,96,768]{4,3,2,1,0:T(8,128)(2,1)}, f32[16,768]{1,0:T(8,128)}) custom-call(bf16[256,768]{1,0:T(8,128)(2,1)} %refs_0_.1, bf16[256,768]{1,0:T(8,128)(2,1)} %refs_1_.1, bf16[2,2,768]{2,1,0:T(2,128)(2,1)} %refs_2_.1, bf16[2,2,96,768]{3,2,1,0:T(8,128)(2,1)} %bitcast.16, ...), custom_call_target="tpu_custom_call" | custom-call | tf_op jit(solution)/shard_map/layers/pallas_call | solution.py:1019
  215.3 7.0 %finish.1 = (bf16[256,768]{1,0:T(8,128)(2,1)}, bf16[256,768]{1,0:T(8,128)(2,1)}, f32[2,2,192]{2,1,0:T(2,128)}, f32[2,2,96,768]{3,2,1,0:T(8,128)}, f32[2,2,48,768...) custom-call(bf16[256,768]{1,0:T(8,128)(2,1)} %get-tuple-element.28.o, ...), custom_call_target="tpu_custom_call" | custom-call | tf_op jit(solution)/shard_map/finish/pallas_call | solution.py:1060

commit v7 on v6

--- a/solution.py
+++ b/solution.py
@@ -20,7 +20,7 @@
 CHUNKS = 4
 LAG = 2
 PACE = (
-    dict(feed=(1, 0, 0, 0, 1, 0, 0, 1), feed_end=0, ffn_end=1, mix=(1, 0, 1, 0, 1, 1, 1, 1), scan=(0, 0, 1, 1, 0, 1, 1, 0), end=1),
+    dict(feed=(0, 0, 0, 0, 1, 0, 0, 1), feed_end=0, ffn_end=1, mix=(1, 0, 1, 0, 1, 1, 1, 1), scan=(0, 0, 1, 1, 0, 1, 1, 0), end=1),
     dict(feed=(1, 1, 1, 0, 1, 0, 0, 1), feed_end=1, ffn_end=2, mix=(1, 0, 1, 0, 1, 1, 1, 1), scan=(0, 1, 0, 1, 1, 0, 1, 0), end=2),
 )
 AHEAD = 6
@@ -769,7 +769,18 @@
                 full[xi, c, core] = r.grad[c].astype(BF16)
                 ag_start(e, full, c)
 
+        def down_grad():
+            part = mm_tn(flat(r.hidden[l]), flat(full[...])).astype(BF16)
+            r.wg[l, n_ffn - z.fu : n_ffn] = part.reshape(z.fu, 2, z.blk, D)
+
         def feed_back(j):
+            if step == 0:
+
+                @pl.when(j == 0)
+                def _():
+                    down_grad()
+                    ticks(2, base + 4)
+
             chip, c = chip_chunk(j, descending, step > 0)
             g_hidden = mm_nt(flat(full[chip, c]), r.wdown[l])
             both = flat(r.gup[l, chip, c]).astype(F32)
@@ -783,10 +794,11 @@
 
             rs_step(e, j, descending, step > 0)
 
-            @pl.when(j == (2 * N - 1 if step > 0 else 0))
-            def _():
-                part = mm_tn(flat(r.hidden[l]), flat(full[...])).astype(BF16)
-                r.wg[l, n_ffn - z.fu : n_ffn] = part.reshape(z.fu, 2, z.blk, D)
+            if step > 0:
+
+                @pl.when(j == 2 * N - 1)
+                def _():
+                    down_grad()
 
             ticks_in_loop(j, pace["feed"], lambda at: base + (4 if step == 0 or at == 2 * N - 1 else 0))
 

time: 223 us -> 222 us (level)
  no operation moved by 1% of the time
where the time goes in v7:
time: 222 us
  Pallas kernels  221 us (100%)
    pallas_call x1, Pallas kernels, local(): pl.pallas_call(functools.partial(mega, z, names), out_shape=(shape(x.shap...  214 us
    pallas_call x1, Pallas kernels, local(): pl.pallas_call(functools.partial(finish, z, n_tensor), grid=(L, G), out_s...  7.04 us

profile of v7, /device:TPU:0, one launch (start us, length us, event | category | flops | bytes accessed | tf_op | source)
XLA Modules:
  0.0 222.1 jit_solution(18005471270106545263)
XLA Ops:
  0.6 214.2 %layers.1 = (bf16[256,768]{1,0:T(8,128)(2,1)}, bf16[256,768]{1,0:T(8,128)(2,1)}, bf16[2,10,2,96,768]{4,3,2,1,0:T(8,128)(2,1)}, f32[16,768]{1,0:T(8,128)}) custom-call(bf16[256,768]{1,0:T(8,128)(2,1)} %refs_0_.1, bf16[256,768]{1,0:T(8,128)(2,1)} %refs_1_.1, bf16[2,2,768]{2,1,0:T(2,128)(2,1)} %refs_2_.1, bf16[2,2,96,768]{3,2,1,0:T(8,128)(2,1)} %bitcast.16, ...), custom_call_target="tpu_custom_call" | custom-call | tf_op jit(solution)/shard_map/layers/pallas_call | solution.py:1031
  214.9 7.0 %finish.1 = (bf16[256,768]{1,0:T(8,128)(2,1)}, bf16[256,768]{1,0:T(8,128)(2,1)}, f32[2,2,192]{2,1,0:T(2,128)}, f32[2,2,96,768]{3,2,1,0:T(8,128)}, f32[2,2,48,768...) custom-call(bf16[256,768]{1,0:T(8,128)(2,1)} %get-tuple-element.28.o, ...), custom_call_target="tpu_custom_call" | custom-call | tf_op jit(solution)/shard_map/finish/pallas_call | solution.py:1072
